TPU v7x, 128 devices: a whole 4x4x4 slice. The times are simulated.
128 devices in a mesh: seq: 8 (over y_lo, x), ctx: 16 (over y_hi, z, core).
Axes of the slice: x: 4, y: 4 (y_hi: 2, y_lo: 2; y = y_hi * 2 + y_lo), z: 4, core: 2. Of those that a mesh axis runs over, the one named last changes fastest.
Arguments:
- tokens: bfloat16 [8, 3072, 1024], P('seq', 'ctx'), may hold values from -6 to 6
- cotangent: bfloat16 [8, 3072, 1024], P('seq', 'ctx'), may hold values from -6 to 6
- w_query: bfloat16 [1024, 1024], P('seq'), may hold values from -0.1875 to 0.1875
- b_query: bfloat16 [1024], P('seq'), may hold values from -3 to 3
- w_key: bfloat16 [1024, 1024], P('seq'), may hold values from -0.1875 to 0.1875
- w_value: bfloat16 [1024, 1024], P('seq'), may hold values from -0.1875 to 0.1875
- b_value: bfloat16 [1024], P('seq'), may hold values from -3 to 3
- w_output: bfloat16 [1024, 1024], P('seq'), may hold values from -2.5 to 2.5
- b_output: bfloat16 [1024], P('seq'), may hold values from -3 to 3
- first_gain: bfloat16 [1024], P('seq'), may hold values from 0.5 to 1.5
- first_shift: bfloat16 [1024], P('seq'), may hold values from -3 to 3
- w_inner: bfloat16 [1024, 4096], P('seq'), may hold values from -0.1875 to 0.1875
- b_inner: bfloat16 [4096], P('seq'), may hold values from -3 to 3
- w_outer: bfloat16 [4096, 1024], P('seq'), may hold values from -0.09375 to 0.09375
- b_outer: bfloat16 [1024], P('seq'), may hold values from -3 to 3
- second_gain: bfloat16 [1024], P('seq'), may hold values from 0.5 to 1.5
- second_shift: bfloat16 [1024], P('seq'), may hold values from -3 to 3
Outputs:
- result: bfloat16 [8, 3072, 1024], P('seq', 'ctx')
- token_grad: float32 [8, 3072, 1024], P('seq', 'ctx')
- query_weight_grad: float32 [1024, 1024], P('seq')
- query_bias_grad: float32 [1024], P('seq')
- key_weight_grad: float32 [1024, 1024], P('seq')
- value_weight_grad: float32 [1024, 1024], P('seq')
- value_bias_grad: float32 [1024], P('seq')
- output_weight_grad: float32 [1024, 1024], P('seq')
- output_bias_grad: float32 [1024], P('seq')
- first_gain_grad: float32 [1024], P('seq')
- first_shift_grad: float32 [1024], P('seq')
- inner_weight_grad: float32 [1024, 4096], P('seq')
- inner_bias_grad: float32 [4096], P('seq')
- outer_weight_grad: float32 [4096, 1024], P('seq')
- outer_bias_grad: float32 [1024], P('seq')
- second_gain_grad: float32 [1024], P('seq')
- second_shift_grad: float32 [1024], P('seq')
All inputs are finite; a program needn't handle non-finite values.
Results may differ from a plain program's by a relative error of at most 0.028.
Values may be sent and summed in bfloat16 or wider, within the bound.
A program may use at most 192 MiB of HBM per device.

v0:
```python
import jax
import jax.numpy as jnp
from jax import lax
from jax.sharding import PartitionSpec as P

D = 1024
HEADS = 16
HD = 64


def product(left, right):
    return jnp.dot(left, right, preferred_element_type=jnp.float32)


def product_tn(left, right):
    return lax.dot_general(
        left, right, (((0,), (0,)), ((), ())), preferred_element_type=jnp.float32
    )


def product_nt(left, right):
    return lax.dot_general(
        left, right, (((1,), (1,)), ((), ())), preferred_element_type=jnp.float32
    )


def normalize(hidden, gain, shift):
    centered = hidden - jnp.mean(hidden, axis=-1, keepdims=True)
    inverse = lax.rsqrt(jnp.mean(centered * centered, axis=-1, keepdims=True) + 1e-05)
    normed = centered * inverse
    return (normed * gain.astype(jnp.float32) + shift.astype(jnp.float32), normed, inverse)


def normalize_back(upstream, normed, inverse, gain):
    scaled = upstream * gain.astype(jnp.float32)
    inner = (
        scaled
        - jnp.mean(scaled, axis=-1, keepdims=True)
        - normed * jnp.mean(scaled * normed, axis=-1, keepdims=True)
    )
    return (inverse * inner, jnp.sum(upstream * normed, axis=0), jnp.sum(upstream, axis=0))


def gelu_exact(value):
    return jax.nn.gelu(value, approximate=False)


def key_block(length):
    return max((divisor for divisor in range(1, 1025) if length % divisor == 0))


def per_device(
    tokens,
    cotangent,
    w_query,
    b_query,
    w_key,
    w_value,
    b_value,
    w_output,
    b_output,
    first_gain,
    first_shift,
    w_inner,
    b_inner,
    w_outer,
    b_outer,
    second_gain,
    second_shift,
):
    scale = HD ** (-0.5)
    (
        query_weight,
        query_bias,
        key_weight,
        value_weight,
        value_bias,
        output_weight,
        output_bias,
        norm_gain,
        norm_shift,
        inner_weight,
        inner_bias,
        outer_weight,
        outer_bias,
        final_gain,
        final_shift,
    ) = (
        lax.all_gather(w_query, "seq", axis=0, tiled=True),
        lax.all_gather(b_query, "seq", axis=0, tiled=True),
        lax.all_gather(w_key, "seq", axis=0, tiled=True),
        lax.all_gather(w_value, "seq", axis=0, tiled=True),
        lax.all_gather(b_value, "seq", axis=0, tiled=True),
        lax.all_gather(w_output, "seq", axis=0, tiled=True),
        lax.all_gather(b_output, "seq", axis=0, tiled=True),
        lax.all_gather(first_gain, "seq", axis=0, tiled=True),
        lax.all_gather(first_shift, "seq", axis=0, tiled=True),
        lax.all_gather(w_inner, "seq", axis=0, tiled=True),
        lax.all_gather(b_inner, "seq", axis=0, tiled=True),
        lax.all_gather(w_outer, "seq", axis=0, tiled=True),
        lax.all_gather(b_outer, "seq", axis=0, tiled=True),
        lax.all_gather(second_gain, "seq", axis=0, tiled=True),
        lax.all_gather(second_shift, "seq", axis=0, tiled=True),
    )
    local_rows = tokens[0]
    row_count = local_rows.shape[0]
    query_rows = (product(local_rows, query_weight) + query_bias.astype(jnp.float32)).astype(
        jnp.bfloat16
    )
    key_rows = product(local_rows, key_weight).astype(jnp.bfloat16)
    value_rows = (product(local_rows, value_weight) + value_bias.astype(jnp.float32)).astype(
        jnp.bfloat16
    )
    query_heads = query_rows.reshape(row_count, HEADS, HD)

    def attend_block(carry, block):
        running_max, running_sum, running_out = carry
        key_heads = block[0].reshape(-1, HEADS, HD)
        value_heads = block[1].reshape(-1, HEADS, HD)
        scores = (
            jnp.einsum("thd,shd->hts", query_heads, key_heads, preferred_element_type=jnp.float32)
            * scale
        )
        new_max = jnp.maximum(running_max, jnp.max(scores, axis=-1))
        factor = jnp.exp(running_max - new_max)
        weights = jnp.exp(scores - new_max[..., None])
        running_sum = running_sum * factor + jnp.sum(weights, axis=-1)
        running_out = running_out * factor[..., None] + jnp.einsum(
            "hts,shd->htd",
            weights.astype(jnp.bfloat16),
            value_heads,
            preferred_element_type=jnp.float32,
        )
        return ((new_max, running_sum, running_out), None)

    start_state = (
        jnp.full((HEADS, row_count), -1e30, jnp.float32),
        jnp.zeros((HEADS, row_count), jnp.float32),
        jnp.zeros((HEADS, row_count, HD), jnp.float32),
    )
    carry = start_state
    pieces = (
        lax.all_gather(key_rows, "ctx", axis=0, tiled=True),
        lax.all_gather(value_rows, "ctx", axis=0, tiled=True),
    )
    length = pieces[0].shape[0]
    block = key_block(length)
    blocks = (
        pieces[0].reshape(length // block, block, D),
        pieces[1].reshape(length // block, block, D),
    )
    carry, ignored = lax.scan(attend_block, carry, blocks)
    top_score, total_weight, summed = carry
    attn_heads = summed / total_weight[..., None]
    log_total = top_score + jnp.log(total_weight)
    attended = jnp.transpose(attn_heads, (1, 0, 2)).reshape(row_count, D)
    attended_low = attended.astype(jnp.bfloat16)
    branch = product(attended_low, output_weight) + output_bias.astype(jnp.float32)
    middle, unit_one, inverse_one = normalize(
        local_rows.astype(jnp.float32) + branch, norm_gain, norm_shift
    )
    middle_low = middle.astype(jnp.bfloat16)
    inner = product(middle_low, inner_weight) + inner_bias.astype(jnp.float32)
    active, gelu_pull = jax.vjp(gelu_exact, inner)
    active_low = active.astype(jnp.bfloat16)
    outer = product(active_low, outer_weight) + outer_bias.astype(jnp.float32)
    result_rows, unit_two, inverse_two = normalize(middle + outer, final_gain, final_shift)
    upstream = cotangent[0].astype(jnp.float32)
    grad_mid, grad_final_gain, grad_final_shift = normalize_back(
        upstream, unit_two, inverse_two, final_gain
    )
    grad_outer_low = grad_mid.astype(jnp.bfloat16)
    grad_outer_weight = product_tn(active_low, grad_outer_low)
    grad_outer_bias = jnp.sum(grad_outer_low.astype(jnp.float32), axis=0)
    grad_active = product_nt(grad_outer_low, outer_weight)
    grad_inner_low = gelu_pull(grad_active)[0].astype(jnp.bfloat16)
    grad_inner_weight = product_tn(middle_low, grad_inner_low)
    grad_inner_bias = jnp.sum(grad_inner_low.astype(jnp.float32), axis=0)
    grad_middle = product_nt(grad_inner_low, inner_weight) + grad_mid
    grad_residual, grad_norm_gain, grad_norm_shift = normalize_back(
        grad_middle, unit_one, inverse_one, norm_gain
    )
    grad_branch_low = grad_residual.astype(jnp.bfloat16)
    grad_output_weight = product_tn(attended_low, grad_branch_low)
    grad_output_bias = jnp.sum(grad_branch_low.astype(jnp.float32), axis=0)
    grad_flat = product_nt(grad_branch_low, output_weight).astype(jnp.bfloat16)
    grad_heads = grad_flat.reshape(row_count, HEADS, HD)
    delta = jnp.einsum("thd,htd->ht", grad_heads.astype(jnp.float32), attn_heads)

    def back_block(grad_query, block):
        key_heads = block[0].reshape(-1, HEADS, HD)
        value_heads = block[1].reshape(-1, HEADS, HD)
        scores = (
            jnp.einsum("thd,shd->hts", query_heads, key_heads, preferred_element_type=jnp.float32)
            * scale
        )
        probs = jnp.exp(scores - log_total[..., None])
        grad_value = jnp.einsum(
            "hts,thd->shd",
            probs.astype(jnp.bfloat16),
            grad_heads,
            preferred_element_type=jnp.float32,
        )
        grad_probs = jnp.einsum(
            "thd,shd->hts", grad_heads, value_heads, preferred_element_type=jnp.float32
        )
        grad_scores = (probs * (grad_probs - delta[..., None])).astype(jnp.bfloat16)
        grad_query = grad_query + jnp.einsum(
            "hts,shd->htd", grad_scores, key_heads, preferred_element_type=jnp.float32
        )
        grad_key = (
            jnp.einsum("hts,thd->shd", grad_scores, query_heads, preferred_element_type=jnp.float32)
            * scale
        )
        return (grad_query, (grad_key.reshape(-1, D), grad_value.reshape(-1, D)))

    pieces = (
        lax.all_gather(key_rows, "ctx", axis=0, tiled=True),
        lax.all_gather(value_rows, "ctx", axis=0, tiled=True),
    )
    grad_query = jnp.zeros((HEADS, row_count, HD), jnp.float32)
    length = pieces[0].shape[0]
    block = key_block(length)
    blocks = (
        pieces[0].reshape(length // block, block, D),
        pieces[1].reshape(length // block, block, D),
    )
    grad_query, (key_parts, value_parts) = lax.scan(back_block, grad_query, blocks)
    key_total = key_parts.reshape(length, D)
    value_total = value_parts.reshape(length, D)
    key_share, value_share = (
        lax.psum_scatter(
            key_total.astype(jnp.bfloat16), "ctx", scatter_dimension=0, tiled=True
        ).astype(jnp.float32),
        lax.psum_scatter(
            value_total.astype(jnp.bfloat16), "ctx", scatter_dimension=0, tiled=True
        ).astype(jnp.float32),
    )
    grad_query_low = (jnp.transpose(grad_query, (1, 0, 2)).reshape(row_count, D) * scale).astype(
        jnp.bfloat16
    )
    grad_key_low = key_share.astype(jnp.bfloat16)
    grad_value_low = value_share.astype(jnp.bfloat16)
    grad_query_weight = product_tn(local_rows, grad_query_low)
    grad_query_bias = jnp.sum(grad_query_low.astype(jnp.float32), axis=0)
    grad_key_weight = product_tn(local_rows, grad_key_low)
    grad_value_weight = product_tn(local_rows, grad_value_low)
    grad_value_bias = jnp.sum(grad_value_low.astype(jnp.float32), axis=0)
    grad_tokens = (
        grad_residual
        + product_nt(grad_query_low, query_weight)
        + product_nt(grad_key_low, key_weight)
        + product_nt(grad_value_low, value_weight)
    )
    partial_value = (
        lax.psum_scatter(
            grad_query_weight.astype(jnp.bfloat16), "seq", scatter_dimension=0, tiled=True
        ).astype(jnp.float32),
        lax.psum_scatter(
            grad_query_bias.astype(jnp.bfloat16), "seq", scatter_dimension=0, tiled=True
        ).astype(jnp.float32),
        lax.psum_scatter(
            grad_key_weight.astype(jnp.bfloat16), "seq", scatter_dimension=0, tiled=True
        ).astype(jnp.float32),
        lax.psum_scatter(
            grad_value_weight.astype(jnp.bfloat16), "seq", scatter_dimension=0, tiled=True
        ).astype(jnp.float32),
        lax.psum_scatter(
            grad_value_bias.astype(jnp.bfloat16), "seq", scatter_dimension=0, tiled=True
        ).astype(jnp.float32),
        lax.psum_scatter(
            grad_output_weight.astype(jnp.bfloat16), "seq", scatter_dimension=0, tiled=True
        ).astype(jnp.float32),
        lax.psum_scatter(
            grad_output_bias.astype(jnp.bfloat16), "seq", scatter_dimension=0, tiled=True
        ).astype(jnp.float32),
        lax.psum_scatter(
            grad_norm_gain.astype(jnp.bfloat16), "seq", scatter_dimension=0, tiled=True
        ).astype(jnp.float32),
        lax.psum_scatter(
            grad_norm_shift.astype(jnp.bfloat16), "seq", scatter_dimension=0, tiled=True
        ).astype(jnp.float32),
        lax.psum_scatter(
            grad_inner_weight.astype(jnp.bfloat16), "seq", scatter_dimension=0, tiled=True
        ).astype(jnp.float32),
        lax.psum_scatter(
            grad_inner_bias.astype(jnp.bfloat16), "seq", scatter_dimension=0, tiled=True
        ).astype(jnp.float32),
        lax.psum_scatter(
            grad_outer_weight.astype(jnp.bfloat16), "seq", scatter_dimension=0, tiled=True
        ).astype(jnp.float32),
        lax.psum_scatter(
            grad_outer_bias.astype(jnp.bfloat16), "seq", scatter_dimension=0, tiled=True
        ).astype(jnp.float32),
        lax.psum_scatter(
            grad_final_gain.astype(jnp.bfloat16), "seq", scatter_dimension=0, tiled=True
        ).astype(jnp.float32),
        lax.psum_scatter(
            grad_final_shift.astype(jnp.bfloat16), "seq", scatter_dimension=0, tiled=True
        ).astype(jnp.float32),
    )
    shares = (
        lax.psum(partial_value[0].astype(jnp.bfloat16), "ctx").astype(jnp.float32),
        lax.psum(partial_value[1].astype(jnp.bfloat16), "ctx").astype(jnp.float32),
        lax.psum(partial_value[2].astype(jnp.bfloat16), "ctx").astype(jnp.float32),
        lax.psum(partial_value[3].astype(jnp.bfloat16), "ctx").astype(jnp.float32),
        lax.psum(partial_value[4].astype(jnp.bfloat16), "ctx").astype(jnp.float32),
        lax.psum(partial_value[5].astype(jnp.bfloat16), "ctx").astype(jnp.float32),
        lax.psum(partial_value[6].astype(jnp.bfloat16), "ctx").astype(jnp.float32),
        lax.psum(partial_value[7].astype(jnp.bfloat16), "ctx").astype(jnp.float32),
        lax.psum(partial_value[8].astype(jnp.bfloat16), "ctx").astype(jnp.float32),
        lax.psum(partial_value[9].astype(jnp.bfloat16), "ctx").astype(jnp.float32),
        lax.psum(partial_value[10].astype(jnp.bfloat16), "ctx").astype(jnp.float32),
        lax.psum(partial_value[11].astype(jnp.bfloat16), "ctx").astype(jnp.float32),
        lax.psum(partial_value[12].astype(jnp.bfloat16), "ctx").astype(jnp.float32),
        lax.psum(partial_value[13].astype(jnp.bfloat16), "ctx").astype(jnp.float32),
        lax.psum(partial_value[14].astype(jnp.bfloat16), "ctx").astype(jnp.float32),
    )
    return (
        result_rows.astype(jnp.bfloat16)[None],
        grad_tokens[None],
        shares[0],
        shares[1],
        shares[2],
        shares[3],
        shares[4],
        shares[5],
        shares[6],
        shares[7],
        shares[8],
        shares[9],
        shares[10],
        shares[11],
        shares[12],
        shares[13],
        shares[14],
    )


def solution(mesh):
    placed = (
        P("seq", "ctx", None),
        P("seq", "ctx", None),
        P("seq", None),
        P("seq"),
        P("seq", None),
        P("seq", None),
        P("seq"),
        P("seq", None),
        P("seq"),
        P("seq"),
        P("seq"),
        P("seq", None),
        P("seq"),
        P("seq", None),
        P("seq"),
        P("seq"),
        P("seq"),
    )
    return jax.shard_map(
        per_device,
        mesh=mesh,
        in_specs=placed,
        out_specs=(
            P("seq", "ctx", None),
            P("seq", "ctx", None),
            P("seq", None),
            P("seq"),
            P("seq", None),
            P("seq", None),
            P("seq"),
            P("seq", None),
            P("seq"),
            P("seq"),
            P("seq"),
            P("seq", None),
            P("seq"),
            P("seq", None),
            P("seq"),
            P("seq"),
            P("seq"),
        ),
        check_vma=False,
    )
```

profile of v0, /device:TPU:1, one launch (start us, length us, event | category | flops | bytes accessed | tf_op | source)
XLA Modules:
  0.0 1353.7 jit_solution(16434443874671015335)
XLA Ops:
  9.5 39.7 %all-gather.18.cloned.1.call-done = bf16[1024,1024]{1,0:T(8,128)(2,1)} async-done(((bf16[128,1024]{1,0:T(8,128)(2,1)}), bf16[1024,1024]{1,0:T(8,128)(2,1)}) %all-gather.18.cloned.1.call-update) | async-done | bytes 2097168 | tf_op jit(solution)/shard_map/all_gather | solution.py:91
  52.4 14.9 %all-gather.1 = bf16[8,1,128]{2,1,0:T(2,128)(2,1)S(1)} all-gather(bf16[1,1,128]{2,1,0:T(2,128)(2,1)S(1)} %bitcast.203), channel_id=1, replica_groups=mesh['seq'=8,'ctx'=16] {'seq'}, dimensions={0}, use_global_device_ids=true | all-gather | bytes 2304 | tf_op jit(solution)/shard_map/all_gather | solution.py:93
  67.3 24.7 %all-gather.24.cloned.1.call-done = bf16[1024,1024]{1,0:T(8,128)(2,1)} async-done(((bf16[128,1024]{1,0:T(8,128)(2,1)}), bf16[1024,1024]{1,0:T(8,128)(2,1)}) %all-gather.24.cloned.1.call-update) | async-done | bytes 2097168 | tf_op jit(solution)/shard_map/all_gather | solution.py:92
  97.1 14.9 %all-gather.6 = bf16[8,1,128]{2,1,0:T(2,128)(2,1)S(1)} all-gather(bf16[1,1,128]{2,1,0:T(2,128)(2,1)S(1)} %bitcast.204), channel_id=1, replica_groups=mesh['seq'=8,'ctx'=16] {'seq'}, dimensions={0}, use_global_device_ids=true | all-gather | bytes 2304 | tf_op jit(solution)/shard_map/all_gather | solution.py:101
  112.1 21.1 %all-gather.5 = bf16[8,1,512]{2,1,0:T(2,128)(2,1)S(1)} all-gather(bf16[1,1,512]{2,1,0:T(2,128)(2,1)S(1)} %reshape.151), channel_id=1, replica_groups=mesh['seq'=8,'ctx'=16] {'seq'}, dimensions={0}, use_global_device_ids=true | all-gather | bytes 9216 | tf_op jit(solution)/shard_map/all_gather | solution.py:99
  133.2 11.7 all-gather.2
  144.9 13.6 %all-gather = bf16[8,1,128]{2,1,0:T(2,128)(2,1)S(1)} all-gather(bf16[1,1,128]{2,1,0:T(2,128)(2,1)S(1)} %bitcast.206), channel_id=1, replica_groups=mesh['seq'=8,'ctx'=16] {'seq'}, dimensions={0}, use_global_device_ids=true | all-gather | bytes 2304 | tf_op jit(solution)/shard_map/all_gather | solution.py:90
  158.5 11.7 all-gather.4
  170.2 13.8 %all-gather.3 = bf16[8,1,128]{2,1,0:T(2,128)(2,1)S(1)} all-gather(bf16[1,1,128]{2,1,0:T(2,128)(2,1)S(1)} %bitcast.208), channel_id=1, replica_groups=mesh['seq'=8,'ctx'=16] {'seq'}, dimensions={0}, use_global_device_ids=true | all-gather | bytes 2304 | tf_op jit(solution)/shard_map/all_gather | solution.py:96
  183.9 12.2 all-gather.7
  196.1 13.6 %all-gather.8 = bf16[8,1,128]{2,1,0:T(2,128)(2,1)S(1)} all-gather(bf16[1,1,128]{2,1,0:T(2,128)(2,1)S(1)} %bitcast.210), channel_id=1, replica_groups=mesh['seq'=8,'ctx'=16] {'seq'}, dimensions={0}, use_global_device_ids=true | all-gather | bytes 2304 | tf_op jit(solution)/shard_map/all_gather | solution.py:103
  212.1 9.0 copy.56
  221.1 49.9 %all-gather.26.cloned.1.call-done = bf16[3072,1024]{1,0:T(8,128)(2,1)} async-done(((bf16[192,1024]{1,0:T(8,128)(2,1)}), bf16[3072,1024]{1,0:T(8,128)(2,1)}) %all-gather.26.cloned.1.call-update) | async-done | bytes 6291472 | tf_op jit(solution)/shard_map/all_gather | solution.py:144
  271.1 8.7 copy.57
  279.7 70.1 %while.30 = (s32[]{:T(128)}, f32[16,192]{1,0:T(8,128)S(1)}, f32[16,192]{1,0:T(8,128)S(1)}, f32[16,192,64]{1,2,0:T(8,128)}, bf16[3,1024,1024]{1,2,0:T(8,128)(2,1)...) while((s32[]{:T(128)}, f32[16,192]{1,0:T(8,128)S(1)}, ...), condition=%wide.region_3.4_spmd.clone, body=%wide.region_0.3_spmd.clone.sunk | while | flops 831077376 | bytes 58785960 | solution.py:152
  335.6 7.1 fusion.120
  354.0 50.2 %all-gather.30.cloned.1.call-done = bf16[1024,4096]{1,0:T(8,128)(2,1)} async-done(((bf16[128,4096]{1,0:T(8,128)(2,1)}), bf16[1024,4096]{1,0:T(8,128)(2,1)}) %all-gather.30.cloned.1.call-update) | async-done | bytes 8388624 | tf_op jit(solution)/shard_map/all_gather | solution.py:98
  404.2 13.1 multiply_convert_fusion.1
  417.3 79.2 %all-gather.32.cloned.1.call-done = bf16[4096,1024]{1,0:T(8,128)(2,1)} async-done(((bf16[512,1024]{1,0:T(8,128)(2,1)}), bf16[4096,1024]{1,0:T(8,128)(2,1)}) %all-gather.32.cloned.1.call-update) | async-done | bytes 8388624 | tf_op jit(solution)/shard_map/all_gather | solution.py:100
  505.2 9.3 fusion.59
  521.3 119.7 %while.31 = (s32[]{:T(128)}, f32[16,192,64]{1,2,0:T(8,128)}, bf16[3,1024,1024]{2,1,0:T(8,128)(2,1)}, bf16[3,1024,1024]{2,1,0:T(8,128)(2,1)}, bf16[3,1024,1024]{1...) while((s32[]{:T(128)}, f32[16,192,64]{1,2,0:T(8,128)}, ...), condition=%wide.region_13.14_spmd.clone, body=%wide.region_12.13_spmd.clone.sunk | while | flops 2040922112 | bytes 145789104 | solution.py:228
  646.8 81.8 %reduce-scatter.15.cloned.1.call-done = bf16[192,1024]{1,0:T(8,128)(2,1)} async-done(((bf16[3072,1024]{1,0:T(8,128)(2,1)}), bf16[192,1024]{1,0:T(8,128)(2,1)}) %reduce-scatter.15.cloned.1.call-update) | async-done | bytes 393232 | tf_op jit(solution)/shard_map/reduce_scatter | solution.py:232
  733.0 88.8 %reduce-scatter.17.cloned.1.call-done = bf16[192,1024]{1,0:T(8,128)(2,1)} async-done(((bf16[3072,1024]{1,0:T(8,128)(2,1)}), bf16[192,1024]{1,0:T(8,128)(2,1)}) %reduce-scatter.17.cloned.1.call-update) | async-done | bytes 393232 | tf_op jit(solution)/shard_map/reduce_scatter | solution.py:235
  845.6 16.7 %reduce-scatter.25.cloned.1.call-done = bf16[128,1024]{1,0:T(8,128)(2,1)} async-done(((bf16[1024,1024]{1,0:T(8,128)(2,1)}), bf16[128,1024]{1,0:T(8,128)(2,1)}) %reduce-scatter.25.cloned.1.call-update) | async-done | bytes 262160
  864.1 42.4 %reduce-scatter.27.cloned.1.call-done = bf16[128,1024]{1,0:T(8,128)(2,1)} async-done(((bf16[1024,1024]{1,0:T(8,128)(2,1)}), bf16[128,1024]{1,0:T(8,128)(2,1)}) %reduce-scatter.27.cloned.1.call-update) | async-done | bytes 262160
  908.3 42.0 %reduce-scatter.29.cloned.1.call-done = bf16[128,1024]{1,0:T(8,128)(2,1)} async-done(((bf16[1024,1024]{1,0:T(8,128)(2,1)}), bf16[128,1024]{1,0:T(8,128)(2,1)}) %reduce-scatter.29.cloned.1.call-update) | async-done | bytes 262160
  952.1 41.8 %reduce-scatter.19.cloned.1.call-done = bf16[128,1024]{1,0:T(8,128)(2,1)} async-done(((bf16[1024,1024]{1,0:T(8,128)(2,1)}), bf16[128,1024]{1,0:T(8,128)(2,1)}) %reduce-scatter.19.cloned.1.call-update) | async-done | bytes 262160 | tf_op jit(solution)/shard_map/reduce_scatter | solution.py:271
  993.9 98.7 %reduce-scatter.21.cloned.1.call-done = bf16[128,4096]{1,0:T(8,128)(2,1)} async-done(((bf16[1024,4096]{1,0:T(8,128)(2,1)}), bf16[128,4096]{1,0:T(8,128)(2,1)}) %reduce-scatter.21.cloned.1.call-update) | async-done | bytes 1048592 | tf_op jit(solution)/shard_map/reduce_scatter | solution.py:283
  1092.7 93.7 %reduce-scatter.23.cloned.1.call-done = bf16[512,1024]{1,0:T(8,128)(2,1)} async-done(((bf16[4096,1024]{1,0:T(8,128)(2,1)}), bf16[512,1024]{1,0:T(8,128)(2,1)}) %reduce-scatter.23.cloned.1.call-update) | async-done | bytes 1048592 | tf_op jit(solution)/shard_map/reduce_scatter | solution.py:289
  1191.2 25.3 %all-reduce.11 = (bf16[1024]{0:T(1024)(128)(2,1)S(1)}, bf16[1024]{0:T(1024)(128)(2,1)S(1)}, bf16[1024]{0:T(1024)(128)(2,1)S(1)}, bf16[1024]{0:T(1024)(128)(2,1)S...) all-reduce(bf16[1024]{0:T(1024)(128)(2,1)S(1)} %reduce_sum.191, ...), channel_id=5, replica_groups=mesh['seq'=8,'ctx'=16] {'seq'}, use_global_device_ids=true, to_apply=%region_19.20.clone | all-reduce | flops 12288 | bytes 49152
  1217.1 40.0 %all-reduce.9 = (bf16[128]{0:T(256)(128)(2,1)S(1)}, bf16[128]{0:T(256)(128)(2,1)S(1)}, bf16[128]{0:T(256)(128)(2,1)S(1)}, bf16[128]{0:T(256)(128)(2,1)S(1)}, bf1...) all-reduce(bf16[128]{0:T(256)(128)(2,1)S(1)} %dynamic-slice.1, ...), channel_id=1, replica_groups=mesh['seq'=8,'ctx'=16] {'ctx'}, use_global_device_ids=true, to_apply=%region_20.21 | all-reduce | flops 1536 | bytes 6144 | tf_op jit(solution)/shard_map/psum | solution.py:304
  1267.6 68.7 %all-reduce.14.cloned.1.call-done = (bf16[128,1024]{0,1:T(8,128)(2,1)}, bf16[128,1024]{0,1:T(8,128)(2,1)}, bf16[128,1024]{0,1:T(8,128)(2,1)}, bf16[128,1024]{1,0...) async-done(((bf16[128,1024]{0,1:T(8,128)(2,1)}, bf16[128,1024]{0,1:T(8,128)(2,1)}, bf16[128,1024]{0,1:T(8,128)(2,1)}, bf16[128,1024]{1,0:T(8,128)(2,1)}, ...) | async-done | bytes 3145744 | tf_op jit(solution)/shard_map/psum | solution.py:303
  (280 shorter events, 278.5 us)
Async XLA Ops:
  7.2 84.8 %copy-start.9 = (bf16[1,192,1024]{2,1,0:T(8,128)(2,1)S(1)}, bf16[1,192,1024]{2,1,0:T(8,128)(2,1)}, u32[]{:S(2)}) copy-start(bf16[1,192,1024]{2,1,0:T(8,128)(2,1)} %param.21) | copy-start | bytes 1179652
  7.2 42.0 %all-gather.18.cloned.1.call-start = ((), (), s32[]{:S(2)}) async-start(), calls=%async_computation.8 | async-start | bytes 2359296 | tf_op jit(solution)/shard_map/all_gather | solution.py:91
  7.9 84.1 %all-gather.24.cloned.1.call-start = ((), (), s32[]{:S(2)}) async-start(), calls=%async_computation.11 | async-start | bytes 2359296 | tf_op jit(solution)/shard_map/all_gather | solution.py:92
  8.7 201.0 %all-gather.22.cloned.1.call-start = ((), (), s32[]{:S(2)}) async-start(), calls=%async_computation.10 | async-start | bytes 2359296 | tf_op jit(solution)/shard_map/all_gather | solution.py:89
  9.4 202.7 %all-gather.20.cloned.1.call-start = ((), (), s32[]{:S(2)}) async-start(), calls=%async_computation.9 | async-start | bytes 6684672 | tf_op jit(solution)/shard_map/all_gather | solution.py:143
  52.2 59.8 %copy-start.35 = (bf16[512]{0:T(512)(128)(2,1)S(1)}, bf16[512]{0:T(512)(128)(2,1)}, u32[]{:S(2)}) copy-start(bf16[512]{0:T(512)(128)(2,1)} %param.33) | copy-start | bytes 3076
  52.2 81.0 %copy-start.38 = (bf16[128]{0:T(256)(128)(2,1)S(1)}, bf16[128]{0:T(256)(128)(2,1)}, u32[]{:S(2)}) copy-start(bf16[128]{0:T(256)(128)(2,1)} %param.29) | copy-start | bytes 772
  52.2 92.7 %copy-start.39 = (bf16[128]{0:T(256)(128)(2,1)S(1)}, bf16[128]{0:T(256)(128)(2,1)}, u32[]{:S(2)}) copy-start(bf16[128]{0:T(256)(128)(2,1)} %param.24) | copy-start | bytes 772
  52.3 106.2 %copy-start.40 = (bf16[128]{0:T(256)(128)(2,1)S(1)}, bf16[128]{0:T(256)(128)(2,1)}, u32[]{:S(2)}) copy-start(bf16[128]{0:T(256)(128)(2,1)} %param.31) | copy-start | bytes 772
  52.3 117.9 %copy-start.41 = (bf16[128]{0:T(256)(128)(2,1)S(1)}, bf16[128]{0:T(256)(128)(2,1)}, u32[]{:S(2)}) copy-start(bf16[128]{0:T(256)(128)(2,1)} %param.30) | copy-start | bytes 772
  52.3 131.7 %copy-start.42 = (bf16[128]{0:T(256)(128)(2,1)S(1)}, bf16[128]{0:T(256)(128)(2,1)}, u32[]{:S(2)}) copy-start(bf16[128]{0:T(256)(128)(2,1)} %param.36) | copy-start | bytes 772
  52.3 143.8 %copy-start.43 = (bf16[128]{0:T(256)(128)(2,1)S(1)}, bf16[128]{0:T(256)(128)(2,1)}, u32[]{:S(2)}) copy-start(bf16[128]{0:T(256)(128)(2,1)} %param.37) | copy-start | bytes 772
  52.3 218.7 %all-gather.26.cloned.1.call-start = ((), (), s32[]{:S(2)}) async-start(), calls=%async_computation.12 | async-start | bytes 6684672 | tf_op jit(solution)/shard_map/all_gather | solution.py:144
  95.0 256.3 %all-gather.28.cloned.1.call-start = ((), (), s32[]{:S(2)}) async-start(), calls=%async_computation.13 | async-start | bytes 2359296 | tf_op jit(solution)/shard_map/all_gather | solution.py:94
  95.5 308.6 %all-gather.30.cloned.1.call-start = ((), (), s32[]{:S(2)}) async-start(), calls=%async_computation.14 | async-start | bytes 9437184 | tf_op jit(solution)/shard_map/all_gather | solution.py:98
  96.3 400.2 %all-gather.32.cloned.1.call-start = ((), (), s32[]{:S(2)}) async-start(), calls=%async_computation.15 | async-start | bytes 9437184 | tf_op jit(solution)/shard_map/all_gather | solution.py:100
  97.0 631.6 %reduce-scatter.15.cloned.1.call-start = ((), (), s32[]{:S(2)}) async-start(), calls=%async_computation.16 | async-start | bytes 6684672 | tf_op jit(solution)/shard_map/reduce_scatter | solution.py:232
  170.2 326.4 %copy-start.27 = (f32[8,1,128]{2,1,0:T(1,128)}, f32[8,1,128]{2,1,0:T(1,128)S(1)}, u32[]{:S(2)}) copy-start(f32[8,1,128]{2,1,0:T(1,128)S(1)} %convert_element_type.300) | copy-start | bytes 12292
  351.2 66.1 %copy-start.12 = (bf16[16,192,64]{1,2,0:T(8,128)(2,1)}, bf16[16,192,64]{1,2,0:T(8,128)(2,1)S(1)}, u32[]{:S(2)}) copy-start(bf16[16,192,64]{1,2,0:T(8,128)(2,1)S(1)} %fusion.38) | copy-start | bytes 1179652
  353.7 164.5 %copy-start.5 = (f32[192,1024]{1,0:T(8,128)}, f32[192,1024]{1,0:T(8,128)S(1)}, u32[]{:S(2)}) copy-start(f32[192,1024]{1,0:T(8,128)S(1)} %get-tuple-element.358) | copy-start | bytes 2359300
  641.0 180.8 %reduce-scatter.17.cloned.1.call-start = ((), (), s32[]{:S(2)}) async-start(), calls=%async_computation.17 | async-start | bytes 6684672 | tf_op jit(solution)/shard_map/reduce_scatter | solution.py:235
  641.6 220.7 %reduce-scatter.25.cloned.1.call-start = ((), (), s32[]{:S(2)}) async-start(), calls=%async_computation.21 | async-start | bytes 2359296
  646.6 259.9 %reduce-scatter.27.cloned.1.call-start = ((), (), s32[]{:S(2)}) async-start(), calls=%async_computation.22 | async-start | bytes 2359296
  732.9 217.3 %reduce-scatter.29.cloned.1.call-start = ((), (), s32[]{:S(2)}) async-start(), calls=%async_computation.23 | async-start | bytes 2359296
  829.0 165.0 %reduce-scatter.19.cloned.1.call-start = ((), (), s32[]{:S(2)}) async-start(), calls=%async_computation.18 | async-start | bytes 2359296 | tf_op jit(solution)/shard_map/reduce_scatter | solution.py:271
  831.1 261.6 %reduce-scatter.21.cloned.1.call-start = ((), (), s32[]{:S(2)}) async-start(), calls=%async_computation.19 | async-start | bytes 9437184 | tf_op jit(solution)/shard_map/reduce_scatter | solution.py:283
  838.2 348.2 %reduce-scatter.23.cloned.1.call-start = ((), (), s32[]{:S(2)}) async-start(), calls=%async_computation.20 | async-start | bytes 9437184 | tf_op jit(solution)/shard_map/reduce_scatter | solution.py:289
  845.5 341.0 %copy-start.17 = (bf16[1,192,1024]{2,1,0:T(8,128)(2,1)S(1)}, bf16[1,192,1024]{2,1,0:T(8,128)(2,1)}, u32[]{:S(2)}) copy-start(bf16[1,192,1024]{2,1,0:T(8,128)(2,1)} %param.22) | copy-start | bytes 1179652
  845.5 341.1 %copy-start.44 = (u32[128]{0:T(128)S(1)}, u32[128]{0:T(128)}, u32[]{:S(2)}) copy-start(u32[128]{0:T(128)} %constant.123) | copy-start | bytes 1540
  845.5 343.0 %copy-start.15 = (bf16[16,192,64]{1,2,0:T(8,128)(2,1)S(1)}, bf16[16,192,64]{1,2,0:T(8,128)(2,1)}, u32[]{:S(2)}) copy-start(bf16[16,192,64]{1,2,0:T(8,128)(2,1)} %copy-done.14) | copy-start | bytes 1179652
  845.6 490.7 %all-reduce.14.cloned.1.call-start = ((), (), s32[]{:S(2)}) async-start(), calls=%async_computation.24 | async-start | bytes 6291456 | tf_op jit(solution)/shard_map/psum | solution.py:303
  1186.5 75.3 %copy-start.24 = (bf16[192,1024]{1,0:T(8,128)(2,1)S(1)}, bf16[192,1024]{1,0:T(8,128)(2,1)}, u32[]{:S(2)}) copy-start(bf16[192,1024]{1,0:T(8,128)(2,1)} %reduce-scatter.15.cloned.1.call-done) | copy-start | bytes 1179652
  (39 other events, 263.1 us)
Sparse Core Ops, SparseCore 0:
  9.7 39.4 all-gather.17
  50.8 41.1 all-gather.23
  93.7 40.3 all-gather.21
  137.0 69.2 all-gather.19
  209.2 61.8 all-gather.25
  272.6 33.4 all-gather.27
  307.7 96.3 all-gather.29
  405.8 90.6 all-gather.31
  641.1 87.4 reduce-scatter.14
  733.2 88.5 reduce-scatter.16
  824.8 37.4 reduce-scatter.24
  865.1 41.3 reduce-scatter.26
  908.9 41.3 reduce-scatter.28
  952.5 41.3 reduce-scatter.18
  996.2 96.4 reduce-scatter.20
  1094.9 91.4 reduce-scatter.22
  1189.8 146.4 all-reduce.13
where the time goes:
time: 1360 us; the launch traced here: 1350 us
  waiting for transfers between devices  823 us (61%)
  blocking collectives  193 us (14%)
  matrix products  183 us (13%)
  local copies, waits for them, and re-layouts  101 us (7%)
  other arithmetic  36.7 us (3%)
  between operations  16.1 us (1%)
    unnamed x20, waiting for transfers between devices  106 us
    reduce_scatter x1, waiting for transfers between devices, per_device(): lax.psum_scatter(grad_inner_weight.astype(jnp.bfloat16), 'seq', scatter_d...  98.7 us
    reduce_scatter x1, waiting for transfers between devices, per_device(): lax.psum_scatter(grad_outer_weight.astype(jnp.bfloat16), 'seq', scatter_d...  93.7 us
    reduce_scatter x1, waiting for transfers between devices, per_device(): lax.psum_scatter(value_total.astype(jnp.bfloat16), 'ctx', scatter_dimensi...  88.8 us
    reduce_scatter x1, waiting for transfers between devices, per_device(): lax.psum_scatter(key_total.astype(jnp.bfloat16), 'ctx', scatter_dimension...  81.8 us
    all_gather x1, waiting for transfers between devices, per_device(): lax.all_gather(w_outer, 'seq', axis=0, tiled=True)  79.2 us
    psum x1, waiting for transfers between devices, per_device(): lax.psum(partial_value[0].astype(jnp.bfloat16), 'ctx').astype(jnp.float32)  68.7 us
    all_gather x1, waiting for transfers between devices, per_device(): lax.all_gather(w_inner, 'seq', axis=0, tiled=True)  50.2 us
  transfers between devices with their start and end apart: 17, of which 14 were waited for; matrix products, arithmetic and copies ran while one was open for 12% of the time, Pallas kernels for 0%

commit v1 on v0

v1 whole, which is shorter than its diff:
```python
import functools
import math

import jax
import jax.numpy as jnp
from jax import lax
from jax.experimental import pallas as pl
from jax.experimental.pallas import tpu as pltpu
from jax.sharding import PartitionSpec as P

D = 1024
HEADS = 16
HD = 64
FF = 4096
SEQ = 8
CHIPS = 8
ROWS = 192
PAIR = 2 * ROWS
LENGTH = CHIPS * PAIR
SCALE2 = HD ** (-0.5) * math.log2(math.e)
BLOCK = 512
BF = jnp.bfloat16
F32 = jnp.float32
ANY = pl.BlockSpec(memory_space=pl.ANY)
VMEM = pl.BlockSpec(memory_space=pltpu.VMEM)


def dot(left, right, dims=((1,), (0,))):
    return lax.dot_general(left, right, (dims, ((), ())), preferred_element_type=F32)


def group_size(group):
    return 2 if group == "core" else 8


def group_me(group):
    if group == "seq":
        return lax.axis_index("seq")
    ctx = lax.axis_index("ctx")
    return lax.rem(ctx, 2) if group == "core" else lax.div(ctx, 2)


def group_device(group, index):
    seq, ctx = lax.axis_index("seq"), lax.axis_index("ctx")
    if group == "seq":
        return (index, ctx)
    if group == "chip":
        return (seq, index * 2 + lax.rem(ctx, 2))
    return (seq, lax.div(ctx, 2) * 2 + index)


def enter(groups):
    barrier = pltpu.get_barrier_semaphore()
    count = 0
    for group in groups:
        size, me = group_size(group), group_me(group)
        for step in range(1, size):
            pl.semaphore_signal(
                barrier,
                inc=1,
                device_id=group_device(group, lax.rem(me + step, size)),
                device_id_type=pl.DeviceIdType.MESH,
            )
            count += 1
    pl.semaphore_wait(barrier, count)


class Exchange:
    def __init__(self, kind, group, source, target, send, recv, own):
        self.kind, self.group = kind, group
        self.source, self.target = source, target
        self.send, self.recv, self.own = send, recv, own

    def copies(self):
        size, me = group_size(self.group), group_me(self.group)
        made = []
        for step in range(1, size):
            peer = lax.rem(me + step, size)
            piece = self.source if self.kind == "ag" else self.source.at[peer]
            made.append(
                pltpu.make_async_remote_copy(
                    src_ref=piece,
                    dst_ref=self.target.at[me],
                    send_sem=self.send.at[step - 1],
                    recv_sem=self.recv.at[step - 1],
                    device_id=group_device(self.group, peer),
                    device_id_type=pl.DeviceIdType.MESH,
                )
            )
        piece = self.source if self.kind == "ag" else self.source.at[me]
        return made, pltpu.make_async_copy(piece, self.target.at[me], self.own)

    def start(self):
        made, own = self.copies()
        for copy in made:
            copy.start()
        own.start()

    def wait(self):
        made, own = self.copies()
        own.wait()
        for copy in made:
            copy.wait()


def target_shape(kind, group, value):
    shape = value.shape if kind == "a2a" else (group_size(group),) + value.shape
    return jax.ShapeDtypeStruct(shape, value.dtype)


def sems(group):
    count = group_size(group) - 1
    return [
        pltpu.SemaphoreType.DMA((count,)),
        pltpu.SemaphoreType.DMA((count,)),
        pltpu.SemaphoreType.DMA,
    ]


def exchange(identifier, *items):
    number = len(items)

    def kernel(*refs):
        enter(sorted({item[1] for item in items}))
        made = [
            Exchange(
                items[at][0],
                items[at][1],
                refs[at],
                refs[number + at],
                *refs[2 * number + 3 * at : 2 * number + 3 * at + 3],
            )
            for at in range(number)
        ]
        for one in made:
            one.start()
        for one in made:
            one.wait()

    return pl.pallas_call(
        kernel,
        out_shape=[target_shape(*item) for item in items],
        in_specs=[ANY] * number,
        out_specs=[ANY] * number,
        scratch_shapes=[sem for item in items for sem in sems(item[1])],
        compiler_params=pltpu.CompilerParams(
            collective_id=identifier, has_side_effects=True
        ),
        name="exchange%d" % identifier,
    )(*[item[2] for item in items])


def attend_forward(identifier, qkv, extra):
    number = len(extra)

    def kernel(*refs):
        qkv_ref, refs = refs[0], refs[1:]
        extra_in, refs = refs[:number], refs[number:]
        qkv_got, summed_ref, back_ref, stat_ref = refs[:4]
        extra_out, refs = refs[4 : 4 + number], refs[4 + number :]
        query_t, keys, value_t, low, refs = refs[0], refs[1], refs[2], refs[3], refs[4:]
        enter(sorted({"chip"} | {item[1] for item in extra}))
        first = Exchange("a2a", "chip", qkv_ref, qkv_got, *refs[:3])
        last = Exchange("a2a", "chip", low, back_ref, *refs[3:6])
        others = [
            Exchange(*extra[at][:2], extra_in[at], extra_out[at], *refs[6 + 3 * at : 9 + 3 * at])
            for at in range(number)
        ]
        first.start()
        for other in others:
            other.start()
        first.wait()
        for chip in range(CHIPS):
            at = pl.ds(chip * PAIR, PAIR)
            query_t[:, at] = qkv_got[chip, 0:HD, :]
            keys[at, :] = qkv_got[chip, HD : 2 * HD, :].astype(F32).T.astype(BF)
            value_t[:, at] = qkv_got[chip, 2 * HD : 3 * HD, :]

        def one_block(block, carry):
            at = pl.ds(pl.multiple_of(block * BLOCK, BLOCK), BLOCK)
            query = query_t[:, at]
            top = jnp.full((1, BLOCK), -1e30, F32)
            total = jnp.zeros((1, BLOCK), F32)
            summed = jnp.zeros((HD, BLOCK), F32)
            for part in range(LENGTH // BLOCK):
                here = slice(part * BLOCK, (part + 1) * BLOCK)
                scores = dot(keys[here, :], query) * SCALE2
                new_top = jnp.maximum(top, jnp.max(scores, axis=0, keepdims=True))
                factor = jnp.exp2(top - new_top)
                weights = jnp.exp2(scores - new_top)
                total = total * factor + jnp.sum(weights, axis=0, keepdims=True)
                summed = summed * factor + dot(value_t[:, here], weights.astype(BF))
                top = new_top
            summed_ref[:, at] = summed / total
            stat_ref[:, at] = top + jnp.log2(total)
            return carry

        lax.fori_loop(0, LENGTH // BLOCK, one_block, 0)
        for chip in range(CHIPS):
            low[chip] = summed_ref[:, chip * PAIR : (chip + 1) * PAIR].astype(BF)
        last.start()
        last.wait()
        for other in others:
            other.wait()

    return pl.pallas_call(
        kernel,
        out_shape=[
            jax.ShapeDtypeStruct((CHIPS, 3 * HD, PAIR), BF),
            jax.ShapeDtypeStruct((HD, LENGTH), F32),
            jax.ShapeDtypeStruct((CHIPS, HD, PAIR), BF),
            jax.ShapeDtypeStruct((1, LENGTH), F32),
        ]
        + [target_shape(*item) for item in extra],
        in_specs=[VMEM] + [ANY] * number,
        out_specs=[VMEM] * 4 + [ANY] * number,
        scratch_shapes=[
            pltpu.VMEM((HD, LENGTH), BF),
            pltpu.VMEM((LENGTH, HD), BF),
            pltpu.VMEM((HD, LENGTH), BF),
            pltpu.VMEM((CHIPS, HD, PAIR), BF),
        ]
        + sems("chip")
        + sems("chip")
        + [sem for item in extra for sem in sems(item[1])],
        compiler_params=pltpu.CompilerParams(
            collective_id=identifier,
            has_side_effects=True,
            vmem_limit_bytes=40 * 1024 * 1024,
        ),
        name="attend_forward",
    )(qkv, *[item[2] for item in extra])


def attend_backward(identifier, qkv_got, summed, stat, grad, extra):
    number = len(extra)

    def kernel(*refs):
        qkv_ref, summed_ref, stat_ref, grad_ref, refs = *refs[:4], refs[4:]
        extra_in, refs = refs[:number], refs[number:]
        grad_got, back_ref, refs = refs[0], refs[1], refs[2:]
        extra_out, refs = refs[:number], refs[number:]
        query_t, queries, key_t, keys, values, up_t, ups, delta_ref = refs[:8]
        grad_query, grad_key, grad_value, low, refs = *refs[8:12], refs[12:]
        enter(sorted({"chip"} | {item[1] for item in extra}))
        first = Exchange("a2a", "chip", grad_ref, grad_got, *refs[:3])
        last = Exchange("a2a", "chip", low, back_ref, *refs[3:6])
        others = [
            Exchange(*extra[at][:2], extra_in[at], extra_out[at], *refs[6 + 3 * at : 9 + 3 * at])
            for at in range(number)
        ]
        first.start()
        for other in others:
            other.start()
        for chip in range(CHIPS):
            at = pl.ds(chip * PAIR, PAIR)
            query_t[:, at] = qkv_ref[chip, 0:HD, :]
            queries[at, :] = qkv_ref[chip, 0:HD, :].astype(F32).T.astype(BF)
            key_t[:, at] = qkv_ref[chip, HD : 2 * HD, :]
            keys[at, :] = qkv_ref[chip, HD : 2 * HD, :].astype(F32).T.astype(BF)
            values[at, :] = qkv_ref[chip, 2 * HD : 3 * HD, :].astype(F32).T.astype(BF)
        grad_key[...] = jnp.zeros_like(grad_key)
        grad_value[...] = jnp.zeros_like(grad_value)
        first.wait()
        for chip in range(CHIPS):
            at = pl.ds(chip * PAIR, PAIR)
            up = grad_got[chip].astype(F32)
            up_t[:, at] = grad_got[chip]
            ups[at, :] = up.T.astype(BF)
            delta_ref[:, at] = jnp.sum(up * summed_ref[:, at], axis=0, keepdims=True)

        def one_block(block, carry):
            at = pl.ds(pl.multiple_of(block * BLOCK, BLOCK), BLOCK)
            query, up = query_t[:, at], up_t[:, at]
            query_rows, up_rows = queries[at, :], ups[at, :]
            stat, delta = stat_ref[:, at], delta_ref[:, at]
            gathered = jnp.zeros((HD, BLOCK), F32)
            for part in range(LENGTH // BLOCK):
                here = slice(part * BLOCK, (part + 1) * BLOCK)
                scores = dot(keys[here, :], query) * SCALE2
                probs = jnp.exp2(scores - stat)
                grad_value[here, :] += dot(probs.astype(BF), up_rows)
                slope = dot(values[here, :], up) - delta
                grad_scores = (probs * slope).astype(BF)
                grad_key[here, :] += dot(grad_scores, query_rows)
                gathered += dot(key_t[:, here], grad_scores)
            grad_query[:, at] = gathered
            return carry

        lax.fori_loop(0, LENGTH // BLOCK, one_block, 0)
        scale = HD ** (-0.5)
        for chip in range(CHIPS):
            at = slice(chip * PAIR, (chip + 1) * PAIR)
            low[chip, 0:HD, :] = (grad_query[:, at] * scale).astype(BF)
            low[chip, HD : 2 * HD, :] = (grad_key[at, :] * scale).T.astype(BF)
            low[chip, 2 * HD : 3 * HD, :] = grad_value[at, :].T.astype(BF)
        last.start()
        last.wait()
        for other in others:
            other.wait()

    return pl.pallas_call(
        kernel,
        out_shape=[
            jax.ShapeDtypeStruct((CHIPS, HD, PAIR), BF),
            jax.ShapeDtypeStruct((CHIPS, 3 * HD, PAIR), BF),
        ]
        + [target_shape(*item) for item in extra],
        in_specs=[VMEM] * 4 + [ANY] * number,
        out_specs=[VMEM] * 2 + [ANY] * number,
        scratch_shapes=[
            pltpu.VMEM((HD, LENGTH), BF),
            pltpu.VMEM((LENGTH, HD), BF),
            pltpu.VMEM((HD, LENGTH), BF),
            pltpu.VMEM((LENGTH, HD), BF),
            pltpu.VMEM((LENGTH, HD), BF),
            pltpu.VMEM((HD, LENGTH), BF),
            pltpu.VMEM((LENGTH, HD), BF),
            pltpu.VMEM((1, LENGTH), F32),
            pltpu.VMEM((HD, LENGTH), F32),
            pltpu.VMEM((LENGTH, HD), F32),
            pltpu.VMEM((LENGTH, HD), F32),
            pltpu.VMEM((CHIPS, 3 * HD, PAIR), BF),
        ]
        + sems("chip")
        + sems("chip")
        + [sem for item in extra for sem in sems(item[1])],
        compiler_params=pltpu.CompilerParams(
            collective_id=identifier,
            has_side_effects=True,
            vmem_limit_bytes=44 * 1024 * 1024,
        ),
        name="attend_backward",
    )(qkv_got, summed, stat, grad, *[item[2] for item in extra])


def normalize(hidden, gain, shift):
    centered = hidden - jnp.mean(hidden, axis=-1, keepdims=True)
    inverse = lax.rsqrt(jnp.mean(centered * centered, axis=-1, keepdims=True) + 1e-05)
    normed = centered * inverse
    return (normed * gain + shift, normed, inverse)


def normalize_back(upstream, normed, inverse, gain):
    scaled = upstream * gain
    inner = (
        scaled
        - jnp.mean(scaled, axis=-1, keepdims=True)
        - normed * jnp.mean(scaled * normed, axis=-1, keepdims=True)
    )
    return (inverse * inner, jnp.sum(upstream * normed, axis=0), jnp.sum(upstream, axis=0))


def gelu_exact(value):
    return jax.nn.gelu(value, approximate=False)


def per_device(
    tokens,
    cotangent,
    w_query,
    b_query,
    w_key,
    w_value,
    b_value,
    w_output,
    b_output,
    first_gain,
    first_shift,
    w_inner,
    b_inner,
    w_outer,
    b_outer,
    second_gain,
    second_shift,
):
    core = lax.rem(lax.axis_index("ctx"), 2)
    rows = tokens[0]

    def pick(value, axis):
        return lax.dynamic_index_in_dim(value, core, axis, keepdims=False)

    qkv_part = pick(
        jnp.stack([w_query, w_key, w_value]).reshape(3, 128, SEQ, 2, HD), 3
    )
    qkv_part = jnp.transpose(qkv_part, (1, 2, 0, 3)).reshape(128, SEQ * 3 * HD)
    output_part = pick(w_output.reshape(2, HD, D), 0)
    inner_part = pick(w_inner.reshape(128, SEQ, 2, 256), 2).reshape(128, FF // 2)
    outer_part = pick(w_outer.reshape(2, 256, D), 0)
    small_part = jnp.concatenate(
        [
            jnp.stack(
                [b_query, b_value, b_output, first_gain, first_shift, b_outer, second_gain, second_shift]
            ),
            b_inner.reshape(4, 128),
            jnp.zeros((4, 128), BF),
        ]
    )
    qkv_weight, small, rows_pair = exchange(
        0, ("ag", "seq", qkv_part), ("ag", "seq", small_part), ("ag", "core", rows)
    )
    qkv_weight = qkv_weight.reshape(D, SEQ * 3 * HD)
    rows_pair = rows_pair.reshape(PAIR, D)
    small = small.astype(F32)
    query_bias = pick(small[:, 0].reshape(SEQ, 2, HD), 1)
    value_bias = pick(small[:, 1].reshape(SEQ, 2, HD), 1)
    qkv_bias = jnp.stack([query_bias, jnp.zeros_like(query_bias), value_bias], axis=1)
    output_bias, norm_gain, norm_shift, outer_bias, final_gain, final_shift = (
        small[:, at].reshape(D) for at in range(2, 8)
    )
    inner_bias = pick(small[:, 8:12].reshape(SEQ, 2, 256), 1).reshape(FF // 2)

    qkv = (dot(qkv_weight, rows_pair, ((0,), (1,))) + qkv_bias.reshape(-1, 1)).astype(BF)
    qkv_got, summed, attended, stat, output_weight, inner_weight, outer_weight = attend_forward(
        1,
        qkv.reshape(CHIPS, 3 * HD, PAIR),
        [("ag", "seq", output_part), ("ag", "seq", inner_part), ("ag", "seq", outer_part)],
    )
    attended = attended.reshape(D // 2, PAIR)
    output_weight = output_weight.reshape(D // 2, D)
    inner_weight = inner_weight.reshape(D, FF // 2)
    outer_weight = outer_weight.reshape(FF // 2, D)

    def core_sum(identifier, partial):
        (got,) = exchange(identifier, ("a2a", "core", partial.reshape(2, ROWS, D)))
        return got[0] + got[1]

    def core_pair(identifier, value):
        (got,) = exchange(identifier, ("ag", "core", value))
        return got.reshape(PAIR, D)

    branch = core_sum(2, dot(attended, output_weight, ((0,), (0,)))) + output_bias
    middle, unit_one, inverse_one = normalize(rows.astype(F32) + branch, norm_gain, norm_shift)
    middle_pair = core_pair(3, middle.astype(BF))
    inner = dot(middle_pair, inner_weight) + inner_bias
    active, gelu_pull = jax.vjp(gelu_exact, inner)
    active_low = active.astype(BF)
    outer = core_sum(4, dot(active_low, outer_weight)) + outer_bias
    result, unit_two, inverse_two = normalize(middle + outer, final_gain, final_shift)
    upstream = cotangent[0].astype(F32)
    grad_mid, grad_final_gain, grad_final_shift = normalize_back(
        upstream, unit_two, inverse_two, final_gain
    )
    grad_outer_low = grad_mid.astype(BF)
    grad_outer_bias = jnp.sum(grad_outer_low.astype(F32), axis=0)
    grad_outer_pair = core_pair(5, grad_outer_low)
    grad_outer_weight = dot(active_low, grad_outer_pair, ((0,), (0,))).astype(BF)
    grad_active = dot(grad_outer_pair, outer_weight, ((1,), (1,)))
    grad_inner_low = gelu_pull(grad_active)[0].astype(BF)
    grad_inner_weight = dot(middle_pair, grad_inner_low, ((0,), (0,))).astype(BF)
    grad_inner_bias = jnp.sum(grad_inner_low.astype(F32), axis=0)
    grad_middle = core_sum(6, dot(grad_inner_low, inner_weight, ((1,), (1,)))) + grad_mid
    grad_residual, grad_norm_gain, grad_norm_shift = normalize_back(
        grad_middle, unit_one, inverse_one, norm_gain
    )
    grad_branch_low = grad_residual.astype(BF)
    grad_output_bias = jnp.sum(grad_branch_low.astype(F32), axis=0)
    grad_branch_pair = core_pair(7, grad_branch_low)
    grad_output_weight = dot(attended, grad_branch_pair).astype(BF)
    grad_attended = dot(output_weight, grad_branch_pair, ((1,), (1,))).astype(BF)

    ignored, grad_qkv, output_terms, inner_terms, outer_terms = attend_backward(
        8,
        qkv_got,
        summed,
        stat,
        grad_attended.reshape(CHIPS, HD, PAIR),
        [
            ("a2a", "seq", grad_output_weight.reshape(SEQ, HD, D)),
            ("a2a", "seq", grad_inner_weight.reshape(SEQ, 128, FF // 2)),
            ("a2a", "seq", grad_outer_weight.reshape(SEQ, 256, D)),
        ],
    )
    grad_qkv = grad_qkv.reshape(SEQ * 3 * HD, PAIR)
    grad_qkv_weight = dot(rows_pair, grad_qkv, ((0,), (1,))).astype(BF)
    token_part = dot(grad_qkv, qkv_weight, ((0,), (1,)))
    grad_qkv_bias = jnp.sum(grad_qkv.astype(F32), axis=1).reshape(SEQ, 3, HD)

    vectors = jnp.concatenate(
        [
            jnp.stack(
                [
                    grad_output_bias,
                    grad_norm_gain,
                    grad_norm_shift,
                    grad_outer_bias,
                    grad_final_gain,
                    grad_final_shift,
                ]
            )
            .reshape(6, SEQ, 128)
            .transpose(1, 0, 2),
            jnp.concatenate([grad_qkv_bias[:, 0], grad_qkv_bias[:, 2]], axis=1)[:, None],
            grad_inner_bias.reshape(SEQ, 2, 128),
            jnp.zeros((SEQ, 7, 128), F32),
        ],
        axis=1,
    )
    qkv_terms, vector_terms, token_terms = exchange(
        9,
        ("a2a", "seq", grad_qkv_weight.reshape(SEQ, 128, SEQ * 3 * HD)),
        ("a2a", "seq", vectors),
        ("a2a", "core", token_part.reshape(2, ROWS, D)),
    )
    grad_tokens = grad_residual + token_terms[0] + token_terms[1]

    def total(terms):
        return jnp.sum(terms.astype(F32), axis=0).astype(BF).reshape(-1, D)

    shares = jnp.concatenate(
        [total(qkv_terms), total(output_terms), total(inner_terms), total(outer_terms)]
    )
    piece = shares.shape[0] // CHIPS
    share_terms, vector_all = exchange(
        10,
        ("a2a", "chip", shares.reshape(CHIPS, piece, D)),
        ("ag", "chip", jnp.sum(vector_terms, axis=0)),
    )
    own = jnp.sum(share_terms.astype(F32), axis=0).astype(BF)
    vector_own = jnp.sum(vector_all, axis=0)
    (own_all,) = exchange(11, ("ag", "chip", own))
    shares_both, vector_both = exchange(
        12, ("ag", "core", own_all.reshape(-1, D)), ("ag", "core", vector_own)
    )
    q_rows = 128 * SEQ * 3 * HD // D
    grad_qkv_all = shares_both[:, :q_rows].reshape(2, 128, SEQ, 3, HD).astype(F32)
    grad_qkv_all = grad_qkv_all.transpose(3, 1, 2, 0, 4).reshape(3, 128, D)
    at = q_rows
    grad_output_all = shares_both[:, at : at + HD].reshape(128, D).astype(F32)
    at += HD
    grad_inner_all = shares_both[:, at : at + 256].reshape(2, 128, SEQ, 256)
    grad_inner_all = grad_inner_all.transpose(1, 2, 0, 3).reshape(128, FF).astype(F32)
    at += 256
    grad_outer_all = shares_both[:, at : at + 256].reshape(512, D).astype(F32)
    whole = vector_both[0, :6] + vector_both[1, :6]
    grad_query_bias = vector_both[:, 6, :HD].reshape(128)
    grad_value_bias = vector_both[:, 6, HD:].reshape(128)
    grad_inner_bias = vector_both[:, 7:9].reshape(512)
    return (
        result.astype(BF)[None],
        grad_tokens[None],
        grad_qkv_all[0],
        grad_query_bias,
        grad_qkv_all[1],
        grad_qkv_all[2],
        grad_value_bias,
        grad_output_all,
        whole[0],
        whole[1],
        whole[2],
        grad_inner_all,
        grad_inner_bias,
        grad_outer_all,
        whole[3],
        whole[4],
        whole[5],
    )


def solution(mesh):
    row = P("seq", None)
    vector = P("seq")
    placed = P("seq", "ctx", None)
    return jax.shard_map(
        per_device,
        mesh=mesh,
        in_specs=(
            placed,
            placed,
            row,
            vector,
            row,
            row,
            vector,
            row,
            vector,
            vector,
            vector,
            row,
            vector,
            row,
            vector,
            vector,
            vector,
        ),
        out_specs=(
            placed,
            placed,
            row,
            vector,
            row,
            row,
            vector,
            row,
            vector,
            vector,
            vector,
            row,
            vector,
            row,
            vector,
            vector,
            vector,
        ),
        check_vma=False,
    )
```

time: 1360 us -> 748 us (0.55)
  waiting for transfers between devices: 823 us -> 0 us
  Pallas kernels: 0 us -> 596 us
  blocking collectives: 193 us -> 0 us
  matrix products: 183 us -> 53.9 us
  local copies, waits for them, and re-layouts: 101 us -> 53.5 us
  between operations: 16.1 us -> 1.76 us
    pallas_call x0 -> x13, Pallas kernels: none -> 596 us  [the longest x11 319 us: exchange(): pl.pallas_call(kernel, out_shape=[target_shape(*item) for item in items],...]
    reduce_scatter x5 -> x0, waiting for transfers between devices: 405 us -> none  [the longest x1 98.7 us: per_device(): lax.psum_scatter(grad_inner_weight.astype(jnp.bfloat16), 'seq', scatter_d...]
    all_gather x8 -> x0, waiting for transfers between devices: 244 us -> none  [the longest x1 79.2 us: per_device(): lax.all_gather(w_outer, 'seq', axis=0, tiled=True)]
    dot_general x39 -> x12, matrix products: 183 us -> 53.9 us  [dot(): lax.dot_general(left, right, (dims, ((), ())), preferred_element_type=F32)]
    all_gather x9 -> x0, blocking collectives: 127 us -> none  [the longest x1 21.1 us: per_device(): lax.all_gather(b_inner, 'seq', axis=0, tiled=True)]
    unnamed x20 -> x0, waiting for transfers between devices: 106 us -> none
    psum x1 -> x0, waiting for transfers between devices: 68.7 us -> none  [per_device(): lax.psum(partial_value[0].astype(jnp.bfloat16), 'ctx').astype(jnp.float32)]
    psum x1 -> x0, blocking collectives: 40 us -> none  [per_device(): lax.psum(partial_value[1].astype(jnp.bfloat16), 'ctx').astype(jnp.float32)]
  transfers between devices with their start and end apart: 17 -> 0, of which waited for: 14 -> 0; matrix products, arithmetic and copies ran while one was open for 12% -> 0% of each run, Pallas kernels for 0% -> 0%
where the time goes in v1:
time: 748 us; the launch traced here: 744 us
  Pallas kernels  596 us (80%)
  matrix products  53.9 us (7%)
  local copies, waits for them, and re-layouts  53.5 us (7%)
  other arithmetic  39 us (5%)
    pallas_call x11, Pallas kernels, exchange(): pl.pallas_call(kernel, out_shape=[target_shape(*item) for item in items],...  319 us
    pallas_call x1, Pallas kernels, attend_backward(): pl.pallas_call(kernel, out_shape=[jax.ShapeDtypeStruct((CHIPS, HD, PAIR),...  138 us
    pallas_call x1, Pallas kernels, attend_forward(): pl.pallas_call(kernel, out_shape=[jax.ShapeDtypeStruct((CHIPS, 3 * HD, PA...  138 us
    dot_general x12, matrix products, dot(): lax.dot_general(left, right, (dims, ((), ())), preferred_element_type=F32)  53.9 us

profile of v1, /device:TPU:1, one launch (start us, length us, event | category | flops | bytes accessed | tf_op | source)
XLA Modules:
  0.0 744.1 jit_solution(11959265228882307912)
XLA Ops:
  6.6 52.9 %exchange0.1 = (bf16[8,128,1536]{2,1,0:T(8,128)(2,1)}, bf16[8,16,128]{2,1,0:T(8,128)(2,1)}, bf16[2,192,1024]{2,1,0:T(8,128)(2,1)}) custom-call(bf16[128,1536]{1,0:T(8,128)(2,1)} %copy.62.refs_0_, bf16[16,128]{1,0:T(8,128)(2,1)} %concatenate.14.refs_1_, bf16[192,1024]{1,0:T(8,128)(2,1)} %bitcast.189), custom_call_target="tpu_custom_call" | custom-call | tf_op jit(solution)/shard_map/exchange0/pallas_call | solution.py:140
  63.6 5.1 fusion.6
  70.1 3.1 dynamic-slice_reduce_fusion
  73.4 138.2 %attend_forward.1 = (bf16[8,192,384]{2,1,0:T(8,128)(2,1)S(1)}, f32[64,3072]{1,0:T(8,128)S(1)}, bf16[8,64,384]{2,1,0:T(8,128)(2,1)S(1)}, f32[1,3072]{1,0:T(1,128)...) custom-call(bf16[8,192,384]{2,1,0:T(8,128)(2,1)S(1)} %bitcast.179, ...), custom_call_target="tpu_custom_call" | custom-call | tf_op jit(solution)/shard_map/attend_forward/pallas_call | solution.py:206
  216.5 2.7 fusion.43.refs_0_
  219.3 27.4 %exchange2.1 = f32[2,192,1024]{2,1,0:T(8,128)} custom-call(f32[2,192,1024]{2,1,0:T(8,128)} %fusion.43.refs_0_), custom_call_target="tpu_custom_call" | custom-call | tf_op jit(solution)/shard_map/exchange2/pallas_call | solution.py:140
  250.3 13.0 %exchange3.1 = bf16[2,192,1024]{2,1,0:T(8,128)(2,1)} custom-call(bf16[192,1024]{1,0:T(8,128)(2,1)} %fusion.28.refs_0_), custom_call_target="tpu_custom_call" | custom-call | tf_op jit(solution)/shard_map/exchange3/pallas_call | solution.py:140
  263.3 12.1 %multiply_convert_fusion = (bf16[384,2048]{1,0:T(8,128)(2,1)S(1)}, f32[384,2048]{1,0:T(8,128)}, f32[384,2048]{1,0:T(8,128)}) fusion(f32[2048]{0:T(1024)S(1)} %bitcast.245, bf16[384,1024]{1,0:T(8,128)(2,1)} %bitcast.207, bf16[1024,2048]{1,0:T(8,128)(2,1)} %bitcast.183), kind=kOutput, calls=%fused_computation.7 | convolution fusion | flops 1662517248 | bytes 12853248 | tf_op jit(solution)/shard_map/dot_general | solution.py:29
  276.6 3.0 fusion.44.refs_0_
  279.6 25.5 %exchange4.1 = f32[2,192,1024]{2,1,0:T(8,128)} custom-call(f32[2,192,1024]{2,1,0:T(8,128)} %fusion.44.refs_0_), custom_call_target="tpu_custom_call" | custom-call | tf_op jit(solution)/shard_map/exchange4/pallas_call | solution.py:140
  310.4 13.1 %exchange5.1 = bf16[2,192,1024]{2,1,0:T(8,128)(2,1)} custom-call(bf16[192,1024]{1,0:T(8,128)(2,1)} %get-tuple-element.105.refs_0_), custom_call_target="tpu_custom_call" | custom-call | tf_op jit(solution)/shard_map/exchange5/pallas_call | solution.py:140
  323.5 7.1 convert_reduce_fusion
  331.8 3.0 fusion.45.refs_0_
  334.7 25.4 %exchange6.1 = f32[2,192,1024]{2,1,0:T(8,128)} custom-call(f32[2,192,1024]{2,1,0:T(8,128)} %fusion.45.refs_0_), custom_call_target="tpu_custom_call" | custom-call | tf_op jit(solution)/shard_map/exchange6/pallas_call | solution.py:140
  363.7 13.1 %exchange7.1 = bf16[2,192,1024]{2,1,0:T(8,128)(2,1)} custom-call(bf16[192,1024]{1,0:T(8,128)(2,1)} %get-tuple-element.107.refs_0_), custom_call_target="tpu_custom_call" | custom-call | tf_op jit(solution)/shard_map/exchange7/pallas_call | solution.py:140
  380.7 4.4 convolution_convert_fusion.1
  385.1 4.8 convolution_convert_fusion
  389.9 138.3 %attend_backward.1 = (bf16[8,64,384]{2,1,0:T(8,128)(2,1)}, bf16[8,192,384]{2,1,0:T(8,128)(2,1)S(1)}, bf16[8,64,1024]{2,1,0:T(8,128)(2,1)S(1)}, bf16[8,128,2048]{2,1,0:T(8,128)(2,1)S(1)}, bf16[8,256,1024]{2,1,0:T(8,128)(2,1)}) custom-call(bf16[8,192,384]{2,1,0:T(8,128)(2,1)S(1)} %get-tuple-element.45.refs_0_, f32[64,3072]{1,0:T(8,128)S(1)} %copy-done.7, ...), custom_call_target="tpu_custom_call" | custom-call | tf_op jit(solution)/shard_map/attend_backward/pallas_call | solution.py:302
  528.2 3.5 convolution_convert_fusion.2
  534.0 4.4 fusion.46.refs_2_
  538.4 49.1 %exchange9.1 = (bf16[8,128,1536]{2,1,0:T(8,128)(2,1)}, f32[8,16,128]{2,1,0:T(8,128)}, f32[2,192,1024]{2,1,0:T(8,128)}) custom-call(bf16[8,128,1536]{2,1,0:T(8,128)(2,1)} %bitcast.194, f32[8,16,128]{2,1,0:T(8,128)} %maximum_maximum_fusion.refs_1_, f32[2,192,1024]{2,1,0:T(8,128)} %fusion.46.refs_2_), custom_call_target="tpu_custom_call" | custom-call | tf_op jit(solution)/shard_map/exchange9/pallas_call | solution.py:140
  587.6 4.0 fusion.25
  591.6 3.1 reduce_sum.241
  594.7 3.0 reduce_sum.240
  602.8 25.3 %exchange10.1 = (bf16[8,96,1024]{2,1,0:T(8,128)(2,1)}, f32[8,16,128]{2,1,0:T(8,128)}) custom-call(bf16[8,96,1024]{2,1,0:T(8,128)(2,1)} %bitcast.190, f32[16,128]{1,0:T(8,128)} %reduce_sum.242.refs_1_), custom_call_target="tpu_custom_call" | custom-call | tf_op jit(solution)/shard_map/exchange10/pallas_call | solution.py:140
  630.5 19.9 %exchange11.1 = bf16[8,96,1024]{2,1,0:T(8,128)(2,1)} custom-call(bf16[96,1024]{1,0:T(8,128)(2,1)} %reduce_sum.243.refs_0_), custom_call_target="tpu_custom_call" | custom-call | tf_op jit(solution)/shard_map/exchange11/pallas_call | solution.py:140
  651.0 54.6 %exchange12.1 = (bf16[2,768,1024]{2,1,0:T(8,128)(2,1)}, f32[2,16,128]{2,1,0:T(8,128)}) custom-call(bf16[768,1024]{1,0:T(8,128)(2,1)} %bitcast.191, f32[16,128]{1,0:T(8,128)} %reduce_sum.244.refs_1_), custom_call_target="tpu_custom_call" | custom-call | tf_op jit(solution)/shard_map/exchange12/pallas_call | solution.py:140
  707.0 3.3 reshape.447
  710.3 8.1 %fusion.39 = (f32[1,128,8,2,64]{4,0,2,1,3:T(1,128)S(1)}, f32[1,128,8,2,64]{4,0,2,1,3:T(1,128)S(1)}, f32[1,128,8,2,64]{4,0,2,1,3:T(1,128)S(1)}) fusion(f32[3,128,8,2,64]{4,0,2,1,3:T(4,128)} %bitcast.187), kind=kLoop, calls=%fused_computation.114 | loop fusion | bytes 3145728 | tf_op jit(solution)/shard_map/slice | solution.py:545
  729.9 2.9 fusion.40
  734.5 3.3 copy.71
  741.1 2.8 bitcast_convert_fusion
  (178 shorter events, 62.7 us)
Async XLA Ops:
  0.7 72.7 %copy-start = (bf16[512,1024]{1,0:T(8,128)(2,1)S(1)}, bf16[512,1024]{1,0:T(8,128)(2,1)}, u32[]{:S(2)}) copy-start(bf16[512,1024]{1,0:T(8,128)(2,1)} %param.30) | copy-start | bytes 3145732
  0.7 4.6 copy-start.36
  0.7 4.6 copy-start.37
  0.7 4.6 copy-start.38
  0.7 4.6 copy-start.39
  0.7 4.6 copy-start.40
  0.7 4.6 copy-start.41
  0.7 4.6 copy-start.42
  0.7 4.6 copy-start.43
  0.8 4.6 copy-start.35
  63.6 5.1 copy-start.31
  63.6 5.2 copy-start.22
  213.7 33.0 %copy-start.6 = (f32[64,3072]{1,0:T(8,128)}, f32[64,3072]{1,0:T(8,128)S(1)}, u32[]{:S(2)}) copy-start(f32[64,3072]{1,0:T(8,128)S(1)} %get-tuple-element.46.refs_1_) | copy-start | bytes 2359300
  216.5 30.2 %copy-start.28 = (f32[8,1,128]{2,1,0:T(1,128)S(1)}, f32[8,1,128]{2,1,0:T(1,128)}, u32[]{:S(2)}) copy-start(f32[8,1,128]{2,1,0:T(1,128)} %get-tuple-element.125) | copy-start | bytes 12292
  219.3 30.0 %copy-start.26 = (f32[8,1,128]{2,1,0:T(1,128)S(1)}, f32[8,1,128]{2,1,0:T(1,128)}, u32[]{:S(2)}) copy-start(f32[8,1,128]{2,1,0:T(1,128)} %get-tuple-element.123) | copy-start | bytes 12292
  246.7 16.6 %copy-start.34 = (f32[8,1,256]{2,1,0:T(1,128)S(1)}, f32[8,1,256]{2,1,0:T(1,128)}, u32[]{:S(2)}) copy-start(f32[8,1,256]{2,1,0:T(1,128)} %constant_dynamic-slice_fusion) | copy-start | bytes 24580
  263.3 13.3 %copy-start.11 = (bf16[8,256,1024]{2,1,0:T(8,128)(2,1)S(1)}, bf16[8,256,1024]{2,1,0:T(8,128)(2,1)}, u32[]{:S(2)}) copy-start(bf16[8,256,1024]{2,1,0:T(8,128)(2,1)} %copy-done.10) | copy-start | bytes 12582916
  279.6 25.6 %copy-start.13 = (f32[192,1024]{1,0:T(8,128)S(1)}, f32[192,1024]{1,0:T(8,128)}, u32[]{:S(2)}) copy-start(f32[192,1024]{1,0:T(8,128)} %copy-done.12) | copy-start | bytes 2359300
  279.6 25.6 %copy-start.27 = (f32[8,1,128]{2,1,0:T(1,128)S(1)}, f32[8,1,128]{2,1,0:T(1,128)}, u32[]{:S(2)}) copy-start(f32[8,1,128]{2,1,0:T(1,128)} %get-tuple-element.124) | copy-start | bytes 12292
  279.6 27.8 %copy-start.25 = (f32[8,1,128]{2,1,0:T(1,128)S(1)}, f32[8,1,128]{2,1,0:T(1,128)}, u32[]{:S(2)}) copy-start(f32[8,1,128]{2,1,0:T(1,128)} %get-tuple-element.126) | copy-start | bytes 12292
  279.6 27.8 %copy-start.32 = (f32[8,1,128]{2,1,0:T(1,128)S(1)}, f32[8,1,128]{2,1,0:T(1,128)}, u32[]{:S(2)}) copy-start(f32[8,1,128]{2,1,0:T(1,128)} %get-tuple-element.127) | copy-start | bytes 12292
  323.5 8.3 %copy-start.9 = (bf16[8,128,2048]{2,1,0:T(8,128)(2,1)S(1)}, bf16[8,128,2048]{2,1,0:T(8,128)(2,1)}, u32[]{:S(2)}) copy-start(bf16[8,128,2048]{2,1,0:T(8,128)(2,1)} %copy-done.8) | copy-start | bytes 12582916
  363.7 16.9 %copy-start.23 = (bf16[2,192,1024]{2,1,0:T(8,128)(2,1)S(1)}, bf16[2,192,1024]{2,1,0:T(8,128)(2,1)}, u32[]{:S(2)}) copy-start(bf16[2,192,1024]{2,1,0:T(8,128)(2,1)} %exchange3.1) | copy-start | bytes 2359300
  380.7 4.4 copy-start.24
  380.7 4.4 copy-start.46
  385.1 4.8 copy-start.7
  389.9 138.3 %copy-start.44 = (bf16[2,192,1024]{2,1,0:T(8,128)(2,1)S(1)}, bf16[2,192,1024]{2,1,0:T(8,128)(2,1)}, u32[]{:S(2)}) copy-start(bf16[2,192,1024]{2,1,0:T(8,128)(2,1)} %get-tuple-element.39) | copy-start | bytes 2359300
  538.4 49.1 %copy-start.15 = (f32[2,192,1024]{2,1,0:T(8,128)S(1)}, f32[2,192,1024]{2,1,0:T(8,128)}, u32[]{:S(2)}) copy-start(f32[2,192,1024]{2,1,0:T(8,128)} %exchange2.1) | copy-start | bytes 4718596
  538.4 49.2 %copy-start.21 = (bf16[1,192,1024]{2,1,0:T(8,128)(2,1)S(1)}, bf16[1,192,1024]{2,1,0:T(8,128)(2,1)}, u32[]{:S(2)}) copy-start(bf16[1,192,1024]{2,1,0:T(8,128)(2,1)} %param.17) | copy-start | bytes 1179652
  628.1 22.3 %copy-start.30 = (f32[8,16,128]{2,1,0:T(8,128)S(1)}, f32[8,16,128]{2,1,0:T(8,128)}, u32[]{:S(2)}) copy-start(f32[8,16,128]{2,1,0:T(8,128)} %get-tuple-element.56) | copy-start | bytes 196612
  710.3 12.1 %copy-start.33 = (f32[2,16,128]{2,1,0:T(8,128)S(1)}, f32[2,16,128]{2,1,0:T(8,128)}, u32[]{:S(2)}) copy-start(f32[2,16,128]{2,1,0:T(8,128)} %get-tuple-element.58) | copy-start | bytes 49156
  734.5 9.4 %copy-start.1 = (bf16[512,1024]{1,0:T(8,128)(2,1)S(1)}, bf16[512,1024]{1,0:T(8,128)(2,1)}, u32[]{:S(2)}) copy-start(bf16[512,1024]{1,0:T(8,128)(2,1)} %param.30) | copy-start | bytes 3145732
  (17 other events, 44.8 us)

commit v2 on v1

--- a/solution.py
+++ b/solution.py
@@ -66,10 +66,10 @@
 
 
 class Exchange:
-    def __init__(self, kind, group, source, target, send, recv, own):
+    def __init__(self, kind, group, source, target, send, recv, own, own_held):
         self.kind, self.group = kind, group
         self.source, self.target = source, target
-        self.send, self.recv, self.own = send, recv, own
+        self.send, self.recv, self.own, self.own_held = send, recv, own, own_held
 
     def copies(self):
         size, me = group_size(self.group), group_me(self.group)
@@ -88,17 +88,21 @@
                 )
             )
         piece = self.source if self.kind == "ag" else self.source.at[me]
-        return made, pltpu.make_async_copy(piece, self.target.at[me], self.own)
+        own_in = pltpu.make_async_copy(piece, self.own_held, self.own.at[0])
+        own_out = pltpu.make_async_copy(self.own_held, self.target.at[me], self.own.at[1])
+        return made, own_in, own_out
 
     def start(self):
-        made, own = self.copies()
+        made, own_in, own_out = self.copies()
         for copy in made:
             copy.start()
-        own.start()
+        own_in.start()
 
     def wait(self):
-        made, own = self.copies()
-        own.wait()
+        made, own_in, own_out = self.copies()
+        own_in.wait()
+        own_out.start()
+        own_out.wait()
         for copy in made:
             copy.wait()
 
@@ -108,12 +112,16 @@
     return jax.ShapeDtypeStruct(shape, value.dtype)
 
 
-def sems(group):
+SCRATCH = 4
+
+
+def scratch(kind, group, value):
     count = group_size(group) - 1
     return [
         pltpu.SemaphoreType.DMA((count,)),
         pltpu.SemaphoreType.DMA((count,)),
-        pltpu.SemaphoreType.DMA,
+        pltpu.SemaphoreType.DMA((2,)),
+        pltpu.VMEM(value.shape if kind == "ag" else value.shape[1:], value.dtype),
     ]
 
 
@@ -128,7 +136,7 @@
                 items[at][1],
                 refs[at],
                 refs[number + at],
-                *refs[2 * number + 3 * at : 2 * number + 3 * at + 3],
+                *refs[2 * number + SCRATCH * at : 2 * number + SCRATCH * (at + 1)],
             )
             for at in range(number)
         ]
@@ -142,7 +150,7 @@
         out_shape=[target_shape(*item) for item in items],
         in_specs=[ANY] * number,
         out_specs=[ANY] * number,
-        scratch_shapes=[sem for item in items for sem in sems(item[1])],
+        scratch_shapes=[ref for item in items for ref in scratch(*item)],
         compiler_params=pltpu.CompilerParams(
             collective_id=identifier, has_side_effects=True
         ),
@@ -160,10 +168,15 @@
         extra_out, refs = refs[4 : 4 + number], refs[4 + number :]
         query_t, keys, value_t, low, refs = refs[0], refs[1], refs[2], refs[3], refs[4:]
         enter(sorted({"chip"} | {item[1] for item in extra}))
-        first = Exchange("a2a", "chip", qkv_ref, qkv_got, *refs[:3])
-        last = Exchange("a2a", "chip", low, back_ref, *refs[3:6])
+        first = Exchange("a2a", "chip", qkv_ref, qkv_got, *refs[:4])
+        last = Exchange("a2a", "chip", low, back_ref, *refs[4:8])
         others = [
-            Exchange(*extra[at][:2], extra_in[at], extra_out[at], *refs[6 + 3 * at : 9 + 3 * at])
+            Exchange(
+                *extra[at][:2],
+                extra_in[at],
+                extra_out[at],
+                *refs[8 + SCRATCH * at : 8 + SCRATCH * (at + 1)],
+            )
             for at in range(number)
         ]
         first.start()
@@ -220,9 +233,9 @@
             pltpu.VMEM((HD, LENGTH), BF),
             pltpu.VMEM((CHIPS, HD, PAIR), BF),
         ]
-        + sems("chip")
-        + sems("chip")
-        + [sem for item in extra for sem in sems(item[1])],
+        + scratch("a2a", "chip", qkv)
+        + scratch("a2a", "chip", jax.ShapeDtypeStruct((CHIPS, HD, PAIR), BF))
+        + [ref for item in extra for ref in scratch(*item)],
         compiler_params=pltpu.CompilerParams(
             collective_id=identifier,
             has_side_effects=True,
@@ -243,10 +256,15 @@
         query_t, queries, key_t, keys, values, up_t, ups, delta_ref = refs[:8]
         grad_query, grad_key, grad_value, low, refs = *refs[8:12], refs[12:]
         enter(sorted({"chip"} | {item[1] for item in extra}))
-        first = Exchange("a2a", "chip", grad_ref, grad_got, *refs[:3])
-        last = Exchange("a2a", "chip", low, back_ref, *refs[3:6])
+        first = Exchange("a2a", "chip", grad_ref, grad_got, *refs[:4])
+        last = Exchange("a2a", "chip", low, back_ref, *refs[4:8])
         others = [
-            Exchange(*extra[at][:2], extra_in[at], extra_out[at], *refs[6 + 3 * at : 9 + 3 * at])
+            Exchange(
+                *extra[at][:2],
+                extra_in[at],
+                extra_out[at],
+                *refs[8 + SCRATCH * at : 8 + SCRATCH * (at + 1)],
+            )
             for at in range(number)
         ]
         first.start()
@@ -322,9 +340,9 @@
             pltpu.VMEM((LENGTH, HD), F32),
             pltpu.VMEM((CHIPS, 3 * HD, PAIR), BF),
         ]
-        + sems("chip")
-        + sems("chip")
-        + [sem for item in extra for sem in sems(item[1])],
+        + scratch("a2a", "chip", grad)
+        + scratch("a2a", "chip", qkv_got)
+        + [ref for item in extra for ref in scratch(*item)],
         compiler_params=pltpu.CompilerParams(
             collective_id=identifier,
             has_side_effects=True,

time: 748 us -> 608 us (0.81)
  Pallas kernels: 596 us -> 456 us
    pallas_call x11, Pallas kernels: 319 us -> 179 us  [exchange(): pl.pallas_call(kernel, out_shape=[target_shape(*item) for item in items],...]
where the time goes in v2:
time: 608 us; the launch traced here: 604 us
  Pallas kernels  456 us (75%)
  matrix products  53.6 us (9%)
  local copies, waits for them, and re-layouts  53.5 us (9%)
  other arithmetic  39 us (6%)
    pallas_call x11, Pallas kernels, exchange(): pl.pallas_call(kernel, out_shape=[target_shape(*item) for item in items],...  179 us
    pallas_call x1, Pallas kernels, attend_backward(): pl.pallas_call(kernel, out_shape=[jax.ShapeDtypeStruct((CHIPS, HD, PAIR),...  140 us
    pallas_call x1, Pallas kernels, attend_forward(): pl.pallas_call(kernel, out_shape=[jax.ShapeDtypeStruct((CHIPS, 3 * HD, PA...  137 us
    dot_general x12, matrix products, dot(): lax.dot_general(left, right, (dims, ((), ())), preferred_element_type=F32)  53.6 us
    unnamed x105, local copies, waits for them, and re-layouts  14.9 us

profile of v2, /device:TPU:1, one launch (start us, length us, event | category | flops | bytes accessed | tf_op | source)
XLA Modules:
  0.0 603.8 jit_solution(5056135229820574722)
XLA Ops:
  6.6 54.0 %exchange0.1 = (bf16[8,128,1536]{2,1,0:T(8,128)(2,1)}, bf16[8,16,128]{2,1,0:T(8,128)(2,1)}, bf16[2,192,1024]{2,1,0:T(8,128)(2,1)}) custom-call(bf16[128,1536]{1,0:T(8,128)(2,1)} %copy.62.refs_0_, bf16[16,128]{1,0:T(8,128)(2,1)} %concatenate.14.refs_1_, bf16[192,1024]{1,0:T(8,128)(2,1)} %bitcast.189), custom_call_target="tpu_custom_call" | custom-call | tf_op jit(solution)/shard_map/exchange0/pallas_call | solution.py:148
  64.7 5.1 fusion.6
  71.2 3.1 dynamic-slice_reduce_fusion
  74.5 136.9 %attend_forward.1 = (bf16[8,192,384]{2,1,0:T(8,128)(2,1)S(1)}, f32[64,3072]{1,0:T(8,128)S(1)}, bf16[8,64,384]{2,1,0:T(8,128)(2,1)S(1)}, f32[1,3072]{1,0:T(1,128)...) custom-call(bf16[8,192,384]{2,1,0:T(8,128)(2,1)S(1)} %bitcast.179, ...), custom_call_target="tpu_custom_call" | custom-call | tf_op jit(solution)/shard_map/attend_forward/pallas_call | solution.py:219
  216.3 2.7 fusion.43.refs_0_
  219.0 4.9 exchange2.1
  229.7 12.1 %multiply_convert_fusion = (bf16[384,2048]{1,0:T(8,128)(2,1)S(1)}, f32[384,2048]{1,0:T(8,128)}, f32[384,2048]{1,0:T(8,128)}) fusion(f32[2048]{0:T(1024)S(1)} %bitcast.245, bf16[384,1024]{1,0:T(8,128)(2,1)} %bitcast.207, bf16[1024,2048]{1,0:T(8,128)(2,1)} %bitcast.183), kind=kOutput, calls=%fused_computation.7 | convolution fusion | flops 1662517248 | bytes 12853248 | tf_op jit(solution)/shard_map/dot_general | solution.py:29
  243.0 3.0 fusion.44.refs_0_
  246.0 2.7 exchange4.1
  256.1 7.1 %convert_reduce_fusion = (f32[2048]{0:T(1024)S(1)}, bf16[384,2048]{1,0:T(8,128)(2,1)S(1)}) fusion(f32[384,2048]{1,0:T(8,128)} %get-tuple-element.114, f32[384,2048]{1,0:T(8,128)} %get-tuple-element.136, bf16[384,1024]{1,0:T(8,128)(2,1)} %bitcast.209, bf16[2048,1024]{1,0:T(8,128)(2,1)} %bitcast.185), kind=kOutput, calls=%fused_computation.5 | convolution fusion | flops 1623193600 | bytes 12853248 | tf_op jit(solution)/shard_map/dot_general | solution.py:29
  264.4 3.0 fusion.45.refs_0_
  267.4 2.7 exchange6.1
  270.1 2.5 multiply_reduce_fusion
  279.6 4.4 convolution_convert_fusion.1
  284.4 4.4 convolution_convert_fusion
  288.8 140.0 %attend_backward.1 = (bf16[8,64,384]{2,1,0:T(8,128)(2,1)}, bf16[8,192,384]{2,1,0:T(8,128)(2,1)S(1)}, bf16[8,64,1024]{2,1,0:T(8,128)(2,1)S(1)}, bf16[8,128,2048]{2,1,0:T(8,128)(2,1)S(1)}, bf16[8,256,1024]{2,1,0:T(8,128)(2,1)}) custom-call(bf16[8,192,384]{2,1,0:T(8,128)(2,1)S(1)} %get-tuple-element.45.refs_0_, f32[64,3072]{1,0:T(8,128)S(1)} %copy-done.7, ...), custom_call_target="tpu_custom_call" | custom-call | tf_op jit(solution)/shard_map/attend_backward/pallas_call | solution.py:320
  428.9 3.5 convolution_convert_fusion.2
  434.6 4.4 fusion.46.refs_2_
  439.1 50.5 %exchange9.1 = (bf16[8,128,1536]{2,1,0:T(8,128)(2,1)}, f32[8,16,128]{2,1,0:T(8,128)}, f32[2,192,1024]{2,1,0:T(8,128)}) custom-call(bf16[8,128,1536]{2,1,0:T(8,128)(2,1)} %bitcast.194, f32[8,16,128]{2,1,0:T(8,128)} %maximum_maximum_fusion.refs_1_, f32[2,192,1024]{2,1,0:T(8,128)} %fusion.46.refs_2_), custom_call_target="tpu_custom_call" | custom-call | tf_op jit(solution)/shard_map/exchange9/pallas_call | solution.py:148
  489.6 4.0 fusion.25
  493.6 3.1 reduce_sum.241
  496.7 3.0 reduce_sum.240
  500.1 2.5 reduce_sum.238
  504.7 27.5 %exchange10.1 = (bf16[8,96,1024]{2,1,0:T(8,128)(2,1)}, f32[8,16,128]{2,1,0:T(8,128)}) custom-call(bf16[8,96,1024]{2,1,0:T(8,128)(2,1)} %bitcast.190, f32[16,128]{1,0:T(8,128)} %reduce_sum.242.refs_1_), custom_call_target="tpu_custom_call" | custom-call | tf_op jit(solution)/shard_map/exchange10/pallas_call | solution.py:148
  534.6 20.6 %exchange11.1 = bf16[8,96,1024]{2,1,0:T(8,128)(2,1)} custom-call(bf16[96,1024]{1,0:T(8,128)(2,1)} %reduce_sum.243.refs_0_), custom_call_target="tpu_custom_call" | custom-call | tf_op jit(solution)/shard_map/exchange11/pallas_call | solution.py:148
  555.9 9.4 %exchange12.1 = (bf16[2,768,1024]{2,1,0:T(8,128)(2,1)}, f32[2,16,128]{2,1,0:T(8,128)}) custom-call(bf16[768,1024]{1,0:T(8,128)(2,1)} %bitcast.191, f32[16,128]{1,0:T(8,128)} %reduce_sum.244.refs_1_), custom_call_target="tpu_custom_call" | custom-call | tf_op jit(solution)/shard_map/exchange12/pallas_call | solution.py:148
  566.6 3.3 reshape.447
  569.9 8.1 %fusion.39 = (f32[1,128,8,2,64]{4,0,2,1,3:T(1,128)S(1)}, f32[1,128,8,2,64]{4,0,2,1,3:T(1,128)S(1)}, f32[1,128,8,2,64]{4,0,2,1,3:T(1,128)S(1)}) fusion(f32[3,128,8,2,64]{4,0,2,1,3:T(4,128)} %bitcast.187), kind=kLoop, calls=%fused_computation.114 | loop fusion | bytes 3145728 | tf_op jit(solution)/shard_map/slice | solution.py:563
  589.5 2.9 fusion.40
  594.1 3.3 copy.71
  597.5 2.7 reshape.445
  600.7 2.8 bitcast_convert_fusion
  (178 shorter events, 61.4 us)
Async XLA Ops:
  0.7 73.7 %copy-start = (bf16[512,1024]{1,0:T(8,128)(2,1)S(1)}, bf16[512,1024]{1,0:T(8,128)(2,1)}, u32[]{:S(2)}) copy-start(bf16[512,1024]{1,0:T(8,128)(2,1)} %param.30) | copy-start | bytes 3145732
  0.7 4.6 copy-start.36
  0.7 4.6 copy-start.37
  0.7 4.6 copy-start.38
  0.7 4.6 copy-start.39
  0.7 4.6 copy-start.40
  0.7 4.6 copy-start.41
  0.7 4.6 copy-start.42
  0.7 4.6 copy-start.43
  0.8 4.6 copy-start.35
  64.7 5.1 copy-start.31
  64.7 5.2 copy-start.22
  213.4 10.6 %copy-start.6 = (f32[64,3072]{1,0:T(8,128)}, f32[64,3072]{1,0:T(8,128)S(1)}, u32[]{:S(2)}) copy-start(f32[64,3072]{1,0:T(8,128)S(1)} %get-tuple-element.46.refs_1_) | copy-start | bytes 2359300
  216.3 7.7 %copy-start.28 = (f32[8,1,128]{2,1,0:T(1,128)S(1)}, f32[8,1,128]{2,1,0:T(1,128)}, u32[]{:S(2)}) copy-start(f32[8,1,128]{2,1,0:T(1,128)} %get-tuple-element.125) | copy-start | bytes 12292
  219.0 7.6 %copy-start.26 = (f32[8,1,128]{2,1,0:T(1,128)S(1)}, f32[8,1,128]{2,1,0:T(1,128)}, u32[]{:S(2)}) copy-start(f32[8,1,128]{2,1,0:T(1,128)} %get-tuple-element.123) | copy-start | bytes 12292
  224.0 5.7 copy-start.34
  229.7 13.3 %copy-start.11 = (bf16[8,256,1024]{2,1,0:T(8,128)(2,1)S(1)}, bf16[8,256,1024]{2,1,0:T(8,128)(2,1)}, u32[]{:S(2)}) copy-start(bf16[8,256,1024]{2,1,0:T(8,128)(2,1)} %copy-done.10) | copy-start | bytes 12582916
  246.0 5.0 copy-start.25
  246.0 5.0 copy-start.32
  256.1 8.3 %copy-start.9 = (bf16[8,128,2048]{2,1,0:T(8,128)(2,1)S(1)}, bf16[8,128,2048]{2,1,0:T(8,128)(2,1)}, u32[]{:S(2)}) copy-start(bf16[8,128,2048]{2,1,0:T(8,128)(2,1)} %copy-done.8) | copy-start | bytes 12582916
  273.6 6.0 copy-start.23
  279.6 4.4 copy-start.24
  279.6 4.4 copy-start.46
  284.0 4.8 copy-start.7
  288.8 140.1 %copy-start.44 = (bf16[2,192,1024]{2,1,0:T(8,128)(2,1)S(1)}, bf16[2,192,1024]{2,1,0:T(8,128)(2,1)}, u32[]{:S(2)}) copy-start(bf16[2,192,1024]{2,1,0:T(8,128)(2,1)} %get-tuple-element.39) | copy-start | bytes 2359300
  428.8 4.1 copy-start.19
  439.1 50.5 %copy-start.15 = (f32[2,192,1024]{2,1,0:T(8,128)S(1)}, f32[2,192,1024]{2,1,0:T(8,128)}, u32[]{:S(2)}) copy-start(f32[2,192,1024]{2,1,0:T(8,128)} %exchange2.1) | copy-start | bytes 4718596
  439.1 50.5 %copy-start.21 = (bf16[1,192,1024]{2,1,0:T(8,128)(2,1)S(1)}, bf16[1,192,1024]{2,1,0:T(8,128)(2,1)}, u32[]{:S(2)}) copy-start(bf16[1,192,1024]{2,1,0:T(8,128)(2,1)} %param.17) | copy-start | bytes 1179652
  500.1 4.0 copy-start.29
  532.2 23.1 %copy-start.30 = (f32[8,16,128]{2,1,0:T(8,128)S(1)}, f32[8,16,128]{2,1,0:T(8,128)}, u32[]{:S(2)}) copy-start(f32[8,16,128]{2,1,0:T(8,128)} %get-tuple-element.56) | copy-start | bytes 196612
  569.9 12.1 %copy-start.33 = (f32[2,16,128]{2,1,0:T(8,128)S(1)}, f32[2,16,128]{2,1,0:T(8,128)}, u32[]{:S(2)}) copy-start(f32[2,16,128]{2,1,0:T(8,128)} %get-tuple-element.58) | copy-start | bytes 49156
  594.1 9.4 %copy-start.1 = (bf16[512,1024]{1,0:T(8,128)(2,1)S(1)}, bf16[512,1024]{1,0:T(8,128)(2,1)}, u32[]{:S(2)}) copy-start(bf16[512,1024]{1,0:T(8,128)(2,1)} %param.30) | copy-start | bytes 3145732
  (17 other events, 42.3 us)
